TPU v7x, 32 devices: a whole 2x2x4 slice. The times are simulated.
32 devices in a mesh: slide: 2 (over x), grid: 16 (over z, y, core).
Axes of the slice: x: 2, y: 2, z: 4, core: 2. Of those that a mesh axis runs over, the one named last changes fastest.
Arguments:
- embeddings: bfloat16 [2, 2048, 512], P('slide', 'grid'), may hold values from -6 to 6
- visible: int32 [2, 512], P('slide'), may hold values from 0 to 2047, as said below
- window_id: int32 [2, 2048], P('slide'), may hold values from 0 to 30, as said below
- output_gradient: bfloat16 [2, 2048, 512], P('slide', 'grid'), may hold values from -6 to 6
- mask_token: float32 [512], replicated, may hold values from -4 to 4
- enc_qkv: bfloat16 [512, 1536], replicated, may hold values from -2 to 2
- enc_out: bfloat16 [512, 512], replicated, may hold values from -0.25 to 0.25
- dec_qkv: bfloat16 [512, 1536], replicated, may hold values from -2 to 2
- decoder_projected: bfloat16 [512, 512], replicated, may hold values from -0.25 to 0.25
Outputs:
- grad_embeddings: bfloat16 [2, 2048, 512], P('slide', 'grid')
- grad_enc_out: float32 [512, 512], P('grid', 'slide')
- grad_dec_out: float32 [512, 512], P('grid', 'slide')
Inputs may be any that keep to these rules, and one draw needn't show every extreme that they name: Each row holds 512 different tile numbers in ascending order. Visible tiles come in aligned runs of 32; in every slide all 128 tiles of one block of 128 aligned tiles are visible, and so are the runs that hold tiles 128 - 128 // 2 to 191. `window_id`: window numbers start at 0 in every slide and rise by 0 or 1 from tile to tile; a window holds 1 to 128 consecutive tiles; the last tile of every slide is in window 2 * 16 - 2.
All inputs are finite; a program needn't handle non-finite values.
Results may differ from a plain program's by a relative error of at most 0.019.
Values may be sent and summed in bfloat16 or wider, within the bound.
A program may use at most 64 MiB of HBM per device.

v0:
```python
import math

import jax
import jax.numpy as jnp
from jax import lax
from jax.sharding import PartitionSpec as P

HEADS = 8
WIN = 128


EPS = 1e-06


def shortened(array):

    def short(part):
        return part.astype(jnp.bfloat16) if part.dtype == jnp.float32 else part

    return jax.tree.map(short, array)


def extended_2(block, sides, width):
    for axis, dim in sides:
        count = lax.axis_size(axis)
        forward = [(i, i + 1) for i in range(count - 1)]
        backward = [(target, source) for source, target in forward]
        low = lax.ppermute(
            lax.slice_in_dim(block, block.shape[dim] - width, None, axis=dim), axis, forward
        )
        high = lax.ppermute(lax.slice_in_dim(block, 0, width, axis=dim), axis, backward)
        block = jnp.concatenate([low, block, high], axis=dim)
    return block


def shifted(block, axis, distance):
    devices = range(lax.axis_size(axis))
    route = [(i - distance, i) for i in devices if i - distance in devices]
    return lax.ppermute(block, axis, route)


def rms_f(values):
    return values * lax.rsqrt(jnp.mean(values * values, axis=-1, keepdims=True) + EPS)


def attend(queries, key_vecs, values, allowed, head_count):
    shape_q = queries.shape
    head_width = shape_q[-1] // head_count
    query_per_head = queries.reshape(shape_q[:-1] + (head_count, head_width))
    key_per_head = key_vecs.reshape(key_vecs.shape[:-1] + (head_count, head_width))
    value_per_head = values.reshape(values.shape[:-1] + (head_count, head_width))
    logit_scores = jnp.einsum("...vys,...rys->...yvr", query_per_head, key_per_head) * (
        1.0 / math.sqrt(head_width)
    )
    if allowed is not None:
        logit_scores = jnp.where(allowed[..., None, :, :], logit_scores, -1e30)
    row_top = lax.stop_gradient(jnp.max(logit_scores, axis=-1, keepdims=True))
    weights = jnp.exp(logit_scores - row_top)
    attention_probs = (weights / jnp.sum(weights, axis=-1, keepdims=True)).astype(jnp.bfloat16)
    attention_probs = lax.optimization_barrier(attention_probs).astype(jnp.float32)
    attended_rows = jnp.einsum("...wvy,...ywj->...vwj", attention_probs, value_per_head)
    return attended_rows.reshape(shape_q).astype(jnp.bfloat16)


def encoder_block(tokens, enc_qkv, enc_out):
    width = tokens.shape[-1]
    residual = tokens.astype(jnp.float32)
    normed = rms_f(residual).astype(jnp.bfloat16)
    projected = jnp.dot(normed, enc_qkv, preferred_element_type=jnp.float32).astype(jnp.bfloat16)
    projected = lax.optimization_barrier(projected).astype(jnp.float32)
    attended_rows = attend(
        projected[..., :width],
        projected[..., width : 2 * width],
        projected[..., 2 * width :],
        None,
        HEADS,
    )
    hidden = residual + jnp.dot(attended_rows, enc_out, preferred_element_type=jnp.float32)
    return (hidden.astype(jnp.bfloat16), attended_rows)


def pick_rows(lookup, index_rows):
    return jax.vmap(lambda source_rows, where_at: source_rows[where_at])(lookup, index_rows)


def place_rows(blank, index_rows, updates):
    return jax.vmap(lambda target, where_at, update: target.at[where_at].set(update))(
        blank, index_rows, updates
    )


def back_project(gradient, weight):
    return jnp.einsum(
        "snc,dc->snd",
        gradient,
        weight,
        precision=lax.Precision.HIGHEST,
        preferred_element_type=jnp.float32,
    )


def shards(
    embeddings,
    visible,
    window_id,
    output_gradient,
    mask_token,
    enc_qkv,
    enc_out,
    dec_qkv,
    decoder_projected,
):
    groups = lax.axis_size("grid")
    shard_index = lax.axis_index("grid")
    slides, tile_dev, width = embeddings.shape
    vis_all = visible.shape[1]
    vis_dev = vis_all // groups
    capacity = -(-tile_dev // groups)
    tiles_all = window_id.shape[1]
    slot_count = groups * capacity
    owner_shard = visible // tile_dev
    counts = jnp.sum(
        (owner_shard[:, :, None] == jnp.arange(groups, dtype=jnp.int32)[None, None, :]).astype(
            jnp.int32
        ),
        axis=1,
    )
    before = jnp.cumsum(counts, axis=1) - counts
    own_start = lax.dynamic_index_in_dim(before, shard_index, axis=1, keepdims=False)
    own_count = lax.dynamic_index_in_dim(counts, shard_index, axis=1, keepdims=False)
    peer_ids = jnp.arange(groups, dtype=jnp.int32)[:, None]
    slot_ids = jnp.arange(capacity, dtype=jnp.int32)[None, :]
    start_box = own_start[:, None, None]
    rank_ids = start_box + slot_ids[None] * groups + jnp.mod(peer_ids[None] - start_box, groups)
    is_live = rank_ids < (own_start + own_count)[:, None, None]
    safe_ranks = jnp.minimum(rank_ids, vis_all - 1).reshape(slides, slot_count)
    tile_ids = pick_rows(visible, safe_ranks).reshape(slides, groups, capacity)
    local_rows = jnp.where(is_live, tile_ids - shard_index * tile_dev, tile_dev).reshape(
        slides, slot_count
    )
    my_ranks = jnp.arange(vis_dev, dtype=jnp.int32) * groups + shard_index
    my_tiles = visible[:, my_ranks]
    sources = my_tiles // tile_dev
    source_start = pick_rows(before, sources)
    positions = sources * capacity + (my_ranks[None, :] - source_start) // groups

    def to_slots(values):
        blank = jnp.zeros((slides, slot_count + 1, width), values.dtype)
        return place_rows(blank, positions, values)[:, :slot_count].reshape(
            slides, groups, capacity, width
        )

    def from_tiles(tile_values):
        extended_rows = jnp.concatenate(
            [tile_values, jnp.zeros((slides, 1, width), tile_values.dtype)], axis=1
        )
        return pick_rows(extended_rows, local_rows).reshape(slides, groups, capacity, width)

    arrived = lax.all_to_all(
        from_tiles(embeddings), "grid", split_axis=1, concat_axis=1, tiled=True
    )
    tokens = pick_rows(arrived.reshape(slides, slot_count, width), positions)

    def encode(inputs):
        return encoder_block(inputs, enc_qkv, enc_out)

    encoded, enc_back, encoder_attended = jax.vjp(encode, tokens, has_aux=True)
    returned = lax.all_to_all(
        shortened(to_slots(encoded)), "grid", split_axis=1, concat_axis=1, tiled=True
    )
    base_inputs = jnp.broadcast_to(mask_token, (slides, tile_dev + 1, width))
    inputs = place_rows(
        base_inputs, local_rows, returned.reshape(slides, slot_count, width).astype(jnp.float32)
    )[:, :tile_dev]
    w_query = dec_qkv[:, :width]
    w_keyval = dec_qkv[:, width:]
    normed = rms_f(inputs).astype(jnp.bfloat16)
    queries = jnp.dot(normed, w_query, preferred_element_type=jnp.float32).astype(jnp.bfloat16)
    keyvals = jnp.dot(normed, w_keyval, preferred_element_type=jnp.float32).astype(jnp.bfloat16)
    margin = WIN
    ext_spots = shard_index * tile_dev - margin + jnp.arange(tile_dev + 2 * margin, dtype=jnp.int32)
    inside = (ext_spots >= 0) & (ext_spots < tiles_all)
    ext_ids = jnp.where(inside[None, :], window_id[:, jnp.clip(ext_spots, 0, tiles_all - 1)], -1)
    own_ids = lax.dynamic_slice_in_dim(window_id, shard_index * tile_dev, tile_dev, axis=1)
    extended = extended_2(keyvals, (("grid", 1),), margin)
    queries, extended = lax.optimization_barrier((queries, extended))
    dcontext = jnp.einsum(
        "aph,bh->apb", output_gradient, decoder_projected, preferred_element_type=jnp.float32
    ).astype(jnp.bfloat16)
    block = math.gcd(tile_dev, 256)

    def block_step(carry, index):
        query_block = queries.astype(jnp.float32)
        keyval_block = extended.astype(jnp.float32)
        allowed = own_ids[:, :, None] == ext_ids[:, None, :]

        def window_attend(query_f, keyval_f):
            return attend(query_f, keyval_f[..., :width], keyval_f[..., width:], allowed, HEADS)

        context_block, attn_back = jax.vjp(window_attend, query_block, keyval_block)
        grad_q_block, grad_kv_block = attn_back(dcontext)
        current = carry
        carry = current + grad_kv_block
        return (carry, (grad_q_block, context_block))

    grad_kv, (grad_q_blocks, context_blocks) = lax.scan(
        block_step,
        jnp.zeros((slides, tile_dev + 2 * margin, 2 * width), jnp.float32),
        jnp.arange(tile_dev // block, dtype=jnp.int32),
    )
    grad_q = grad_q_blocks.transpose(1, 0, 2, 3).reshape(slides, tile_dev, width)
    decoder_attended = context_blocks.transpose(1, 0, 2, 3).reshape(slides, tile_dev, width)
    dnormed = back_project(grad_q, w_query)
    from_right = shifted(grad_kv[:, :margin].astype(jnp.bfloat16), "grid", -1).astype(jnp.float32)
    from_left = shifted(grad_kv[:, -margin:].astype(jnp.bfloat16), "grid", 1).astype(jnp.float32)
    middle = grad_kv[:, margin : margin + tile_dev]
    middle = middle.at[:, :margin].add(from_left).at[:, -margin:].add(from_right)
    dnormed = dnormed + back_project(middle, w_keyval)
    _, norm_back = jax.vjp(rms_f, inputs)
    dinputs = norm_back(dnormed)[0] + output_gradient.astype(jnp.float32)
    grad_dec_part = jnp.einsum(
        "qcr,qcu->ru", decoder_attended, output_gradient, preferred_element_type=jnp.float32
    )
    arrived_grads = lax.all_to_all(
        from_tiles(dinputs.astype(jnp.bfloat16)), "grid", split_axis=1, concat_axis=1, tiled=True
    )
    encoded_cotangent = pick_rows(arrived_grads.reshape(slides, slot_count, width), positions)
    grad_enc_part = jnp.einsum(
        "qcr,qcu->ru", encoder_attended, encoded_cotangent, preferred_element_type=jnp.float32
    )
    (dtokens,) = enc_back(encoded_cotangent)
    back_home = lax.all_to_all(
        shortened(to_slots(dtokens)), "grid", split_axis=1, concat_axis=1, tiled=True
    )
    grad_tiles = place_rows(
        jnp.zeros((slides, tile_dev + 1, width), jnp.bfloat16),
        local_rows,
        back_home.reshape(slides, slot_count, width),
    )[:, :tile_dev]
    stacked = jnp.stack([grad_enc_part, grad_dec_part])
    partial_sum = lax.psum_scatter(stacked, "grid", scatter_dimension=1, tiled=True)
    partial_sum = lax.psum_scatter(
        partial_sum.astype(jnp.bfloat16), "slide", scatter_dimension=2, tiled=True
    ).astype(jnp.float32)
    return (grad_tiles, partial_sum[0], partial_sum[1])


def solution(mesh):
    placed = (
        P("slide", "grid", None),
        P("slide", None),
        P("slide", None),
        P("slide", "grid", None),
        P(),
        P(),
        P(),
        P(),
        P(),
    )
    return jax.shard_map(
        shards,
        mesh=mesh,
        in_specs=placed,
        out_specs=(P("slide", "grid", None), P("grid", "slide"), P("grid", "slide")),
        check_vma=False,
    )
```

profile of v0, /device:TPU:0, one launch (start us, length us, event | category | flops | bytes accessed | tf_op | source)
XLA Modules:
  0.0 183.9 jit_solution(3918337503966902945)
XLA Ops:
  7.2 0.8 and_select_fusion
  11.1 1.6 gather_fusion.2
  14.1 0.9 concatenate.13
  15.0 1.8 gather_fusion.4
  16.9 7.4 %all-to-all-start = ((bf16[1,16,8,512]{3,2,0,1:T(8,128)(2,1)}), bf16[1,16,8,512]{3,2,0,1:T(8,128)(2,1)S(1)}, u32[]{:S(2)}, u32[]{:S(2)}) async-start(bf16[1,16,8,512]{3,2,0,1:T(8,128)(2,1)} %bitcast.26), calls=%async_computation | async-start | bytes 262144 | tf_op jit(solution)/shard_map/all_to_all | solution.py:159
  24.3 0.7 gather_fusion
  25.1 0.7 gather_fusion.3
  26.3 2.5 %gather_fusion.1 = s32[384]{0:T(512)S(1)} fusion(s32[2048]{0:T(1024)S(1)} %bitcast.239, s32[1024]{0:T(1024)S(1)} %pad_clamp_fusion), kind=kCustom, calls=%fused_computation.1 | custom fusion | bytes 4608 | tf_op jit(solution)/shard_map/gather | solution.py:183
  28.9 3.3 %all-to-all-done = bf16[1,16,8,512]{3,2,0,1:T(8,128)(2,1)S(1)} async-done(((bf16[1,16,8,512]{3,2,0,1:T(8,128)(2,1)}), bf16[1,16,8,512]{3,2,0,1:T(8,128)(2,1)S(1)}, u32[]{:S(2)}, u32[]{:S(2)}) %all-to-all-start) | async-done | bytes 131104 | tf_op jit(solution)/shard_map/all_to_all | solution.py:159
  32.2 0.7 gather_fusion.5
  35.3 1.1 convert_element_type.219
  36.4 1.2 fusion.21
  37.6 1.5 scatter_custom_fusion
  39.1 1.6 slice_bitcast_fusion.1
  40.7 4.2 %all-to-all-start.1 = ((bf16[1,16,8,512]{3,2,0,1:T(8,128)(2,1)}), bf16[1,16,8,512]{3,2,0,1:T(8,128)(2,1)}, u32[]{:S(2)}, u32[]{:S(2)}) async-start(bf16[1,16,8,512]{3,2,0,1:T(8,128)(2,1)} %slice_bitcast_fusion.1), calls=%async_computation.1 | async-start | bytes 262144 | tf_op jit(solution)/shard_map/all_to_all | solution.py:168
  45.4 2.0 %convolution_convert_fusion.4 = bf16[128,512]{1,0:T(8,128)(2,1)} fusion(bf16[512,512]{1,0:T(8,128)(2,1)} %param.25, bf16[1,128,512]{2,1,0:T(8,128)(2,1)S(1)} %copy-done.8), kind=kOutput, calls=%fused_computation.42 | convolution fusion | flops 67174400 | bytes 786432 | tf_op jit(solution)/shard_map/aph,bh->apb/dot_general | solution.py:187
  47.4 5.4 %all-to-all-done.1 = bf16[1,16,8,512]{3,2,0,1:T(8,128)(2,1)} async-done(((bf16[1,16,8,512]{3,2,0,1:T(8,128)(2,1)}), bf16[1,16,8,512]{3,2,0,1:T(8,128)(2,1)}, u32[]{:S(2)}, u32[]{:S(2)}) %all-to-all-start.1) | async-done | bytes 131104 | tf_op jit(solution)/shard_map/all_to_all | solution.py:168
  52.9 1.5 scatter_custom_fusion.1
  54.5 1.0 fusion.14
  55.6 1.3 collective-permute-start.1
  56.9 3.7 %collective-permute-start = (bf16[1,128,1024]{2,1,0:T(8,128)(2,1)}, bf16[1,128,1024]{2,1,0:T(8,128)(2,1)}, u32[]{:S(2)}, u32[]{:S(2)}) collective-permute-start(bf16[1,128,1024]{2,1,0:T(8,128)(2,1)} %fusion.14), channel_id=1, source_target_pairs={{0,1},{1,2},{2,3},{3,4},{4,5},{5,6},{6,7},{7,8},{8,9},{9,10},{10,1... | collective-permute-start | bytes 786440 | tf_op jit(solution)/shard_map/ppermute | solution.py:28
  60.6 0.7 broadcast_compare_fusion
  61.3 1.7 copy.67
  63.0 0.9 fusion.16
  63.9 1.2 pad_maximum_fusion.1
  66.3 1.3 fusion.13
  67.7 2.7 %fusion.126 = (f32[8,128]{1,0:T(8,128)S(1)}, f32[8,128,384]{2,1,0:T(8,128)}) fusion(bf16[128,8,64]{0,2,1:T(8,128)(2,1)S(1)} %bitcast.262, bf16[384,8,64]{0,2,1:T(8,128)(2,1)S(1)} %bitcast.259, pred[128,384]{1,0:T(8,128)(4,1)} %broadcast_compare_fusion), kind=kOutput, calls=%fused_computation.212 | convolution fusion | flops 51904896 | bytes 2150400 | tf_op jit(solution)/shard_map/while/body/eval_jaxpr/jvp()/sub | solution.py:58
  70.3 1.8 fusion.27
  74.3 3.1 %collective-permute-start.2 = (bf16[1,128,1024]{1,2,0:T(8,128)(2,1)S(1)}, bf16[1,128,1024]{1,2,0:T(8,128)(2,1)S(1)}, u32[]{:S(2)}, u32[]{:S(2)}) collective-permute-start(bf16[1,128,1024]{1,2,0:T(8,128)(2,1)S(1)} %get-tuple-element.76), channel_id=1, source_target_pairs={{0,1},{1,2},{2,3},{3,4},{4,5},{5,6},{6,7},{7,8},{8,9},{9,10},{10,1... | collective-permute-start | bytes 786440 | tf_op jit(solution)/shard_map/ppermute | solution.py:39
  77.4 1.4 collective-permute-start.3
  78.9 0.7 fusion.115
  79.6 0.7 fusion.35
  80.3 2.7 %collective-permute-done.3 = bf16[1,128,1024]{1,2,0:T(8,128)(2,1)S(1)} collective-permute-done((bf16[1,128,1024]{1,2,0:T(8,128)(2,1)S(1)}, bf16[1,128,1024]{1,2,0:T(8,128)(2,1)S(1)}, u32[]{:S(2)}, u32[]{:S(2)}) %collective-permute-start.3) | collective-permute-done | bytes 262176 | tf_op jit(solution)/shard_map/ppermute | solution.py:39
  83.0 1.1 fusion.42
  84.2 1.8 gather_fusion.6
  86.1 8.6 %all-to-all-start.2 = ((bf16[1,16,8,512]{3,2,0,1:T(8,128)(2,1)}), bf16[1,16,8,512]{3,2,0,1:T(8,128)(2,1)S(1)}, u32[]{:S(2)}, u32[]{:S(2)}) async-start(bf16[1,16,8,512]{3,2,0,1:T(8,128)(2,1)} %bitcast.65), calls=%async_computation.2 | async-start | bytes 262144 | tf_op jit(solution)/shard_map/all_to_all | solution.py:224
  95.6 7.0 %all-to-all-done.2 = bf16[1,16,8,512]{3,2,0,1:T(8,128)(2,1)S(1)} async-done(((bf16[1,16,8,512]{3,2,0,1:T(8,128)(2,1)}), bf16[1,16,8,512]{3,2,0,1:T(8,128)(2,1)S(1)}, u32[]{:S(2)}, u32[]{:S(2)}) %all-to-all-start.2) | async-done | bytes 131104 | tf_op jit(solution)/shard_map/all_to_all | solution.py:224
  102.6 0.7 gather_fusion.7
  103.6 1.5 pad_maximum_fusion
  105.2 1.0 copy-done.7
  107.9 0.7 fusion.63
  108.5 0.9 scatter_custom_fusion.2
  110.2 3.5 %all-to-all-start.3 = ((bf16[1,16,8,512]{3,2,0,1:T(8,128)(2,1)}), bf16[1,16,8,512]{3,2,0,1:T(8,128)(2,1)S(1)}, u32[]{:S(2)}, u32[]{:S(2)}) async-start(bf16[1,16,8,512]{3,2,0,1:T(8,128)(2,1)} %slice_bitcast_fusion), calls=%async_computation.3 | async-start | bytes 262144 | tf_op jit(solution)/shard_map/all_to_all | solution.py:232
  113.7 50.8 %reduce-scatter.3.cloned.1.call-done = f32[2,32,512]{2,1,0:T(8,128)} async-done(((f32[2,512,512]{2,1,0:T(8,128)}), f32[2,32,512]{2,1,0:T(8,128)}) %reduce-scatter.3.cloned.1.call-update) | async-done | bytes 131088 | tf_op jit(solution)/shard_map/reduce_scatter | solution.py:241
  164.5 1.5 convert_element_type.252
  166.1 1.2 scatter_custom_fusion.3
  167.9 7.8 %reduce-scatter.5.cloned.1.call-done = bf16[2,32,256]{2,1,0:T(8,128)(2,1)} async-done(((bf16[2,32,512]{2,1,0:T(8,128)(2,1)}), bf16[2,32,256]{2,1,0:T(8,128)(2,1)}) %reduce-scatter.5.cloned.1.call-update) | async-done | bytes 32784 | tf_op jit(solution)/shard_map/reduce_scatter | solution.py:242
  175.7 0.8 convert_element_type.253
  (145 shorter events, 15.2 us)
Async XLA Ops:
  7.2 25.9 %copy-start = (bf16[512,1536]{1,0:T(8,128)(2,1)S(1)}, bf16[512,1536]{1,0:T(8,128)(2,1)}, u32[]{:S(2)}) copy-start(bf16[512,1536]{1,0:T(8,128)(2,1)} %param.22) | copy-start | bytes 4718596
  7.2 17.1 %copy-start.1 = (s32[1,512]{1,0:T(1,128)S(1)}, s32[1,512]{1,0:T(1,128)}, u32[]{:S(2)}) copy-start(s32[1,512]{1,0:T(1,128)} %param.18) | copy-start | bytes 6148
  12.7 13.6 %copy-start.2 = (s32[1,2048]{1,0:T(1,128)S(1)}, s32[1,2048]{1,0:T(1,128)}, u32[]{:S(2)}) copy-start(s32[1,2048]{1,0:T(1,128)} %param.19) | copy-start | bytes 24580
  14.1 38.8 %copy-start.27 = (s32[128]{0:T(128)}, s32[128]{0:T(128)S(1)}, u32[]{:S(2)}) copy-start(s32[128]{0:T(128)S(1)} %get-tuple-element.86) | copy-start | bytes 1540
  16.9 15.3 %all-to-all-start = ((bf16[1,16,8,512]{3,2,0,1:T(8,128)(2,1)}), bf16[1,16,8,512]{3,2,0,1:T(8,128)(2,1)S(1)}, u32[]{:S(2)}, u32[]{:S(2)}) async-start(bf16[1,16,8,512]{3,2,0,1:T(8,128)(2,1)} %bitcast.26), calls=%async_computation | async-start | bytes 262144 | tf_op jit(solution)/shard_map/all_to_all | solution.py:159
  33.4 12.0 %copy-start.8 = (bf16[1,128,512]{2,1,0:T(8,128)(2,1)S(1)}, bf16[1,128,512]{2,1,0:T(8,128)(2,1)}, u32[]{:S(2)}) copy-start(bf16[1,128,512]{2,1,0:T(8,128)(2,1)} %param.20) | copy-start | bytes 393220
  33.7 0.6 copy-start.20
  33.7 19.1 %copy-start.25 = (f32[512]{0:T(512)S(1)}, f32[512]{0:T(512)}, u32[]{:S(2)}) copy-start(f32[512]{0:T(512)} %param.21) | copy-start | bytes 6148
  33.8 0.6 copy-start.22
  34.0 0.6 copy-start.14
  34.1 18.8 %copy-start.11 = (bf16[1,8,32,32]{2,3,1,0:T(8,128)(2,1)}, bf16[1,8,32,32]{2,3,1,0:T(8,128)(2,1)S(1)}, u32[]{:S(2)}) copy-start(bf16[1,8,32,32]{2,3,1,0:T(8,128)(2,1)S(1)} %fusion.69) | copy-start | bytes 49156
  35.3 19.2 %copy-start.4 = (bf16[512,1536]{1,0:T(8,128)(2,1)S(1)}, bf16[512,1536]{1,0:T(8,128)(2,1)}, u32[]{:S(2)}) copy-start(bf16[512,1536]{1,0:T(8,128)(2,1)} %param.24) | copy-start | bytes 4718596
  36.4 16.4 %copy-start.18 = (bf16[32,512]{1,0:T(8,128)(2,1)}, bf16[32,512]{1,0:T(8,128)(2,1)S(1)}, u32[]{:S(2)}) copy-start(bf16[32,512]{1,0:T(8,128)(2,1)S(1)} %convert_element_type.219) | copy-start | bytes 98308
  40.7 12.1 %all-to-all-start.1 = ((bf16[1,16,8,512]{3,2,0,1:T(8,128)(2,1)}), bf16[1,16,8,512]{3,2,0,1:T(8,128)(2,1)}, u32[]{:S(2)}, u32[]{:S(2)}) async-start(bf16[1,16,8,512]{3,2,0,1:T(8,128)(2,1)} %slice_bitcast_fusion.1), calls=%async_computation.1 | async-start | bytes 262144 | tf_op jit(solution)/shard_map/all_to_all | solution.py:168
  54.4 6.2 %copy-start.26 = (s32[128]{0:T(128)S(1)}, s32[128]{0:T(128)}, u32[]{:S(2)}) copy-start(s32[128]{0:T(128)} %dynamic-slice_bitcast_fusion) | copy-start | bytes 1540
  55.6 8.3 %collective-permute-start.1 = (bf16[1,128,1024]{2,1,0:T(8,128)(2,1)}, bf16[1,128,1024]{2,1,0:T(8,128)(2,1)}, u32[]{:S(2)}, u32[]{:S(2)}) collective-permute-start(bf16[1,128,1024]{2,1,0:T(8,128)(2,1)} %fusion.14), channel_id=1, source_target_pairs={{1,0},{2,1},{3,2},{4,3},{5,4},{6,5},{7,6},{8,7},{9,8},{10,9},{11,1... | collective-permute-start | bytes 786440 | tf_op jit(solution)/shard_map/ppermute | solution.py:31
  56.9 7.0 %collective-permute-start = (bf16[1,128,1024]{2,1,0:T(8,128)(2,1)}, bf16[1,128,1024]{2,1,0:T(8,128)(2,1)}, u32[]{:S(2)}, u32[]{:S(2)}) collective-permute-start(bf16[1,128,1024]{2,1,0:T(8,128)(2,1)} %fusion.14), channel_id=1, source_target_pairs={{0,1},{1,2},{2,3},{3,4},{4,5},{5,6},{6,7},{7,8},{8,9},{9,10},{10,1... | collective-permute-start | bytes 786440 | tf_op jit(solution)/shard_map/ppermute | solution.py:28
  65.1 0.9 copy-start.13
  65.1 1.3 copy-start.10
  66.3 4.0 %copy-start.16 = (bf16[1,384,512]{1,2,0:T(8,128)(2,1)}, bf16[1,384,512]{1,2,0:T(8,128)(2,1)S(1)}, u32[]{:S(2)}) copy-start(bf16[1,384,512]{1,2,0:T(8,128)(2,1)S(1)} %copy.76) | copy-start | bytes 1179652
  70.3 1.9 %copy-start.3 = (f32[8,128,384]{2,1,0:T(8,128)S(1)}, f32[8,128,384]{2,1,0:T(8,128)}, u32[]{:S(2)}) copy-start(f32[8,128,384]{2,1,0:T(8,128)} %get-tuple-element.90) | copy-start | bytes 4718596
  70.3 2.1 %copy-start.6 = (bf16[1,8,128,384]{3,2,1,0:T(8,128)(2,1)S(1)}, bf16[1,8,128,384]{3,2,1,0:T(8,128)(2,1)}, u32[]{:S(2)}) copy-start(bf16[1,8,128,384]{3,2,1,0:T(8,128)(2,1)} %fusion.13) | copy-start | bytes 2359300
  72.4 0.8 copy-start.24
  74.1 4.7 %copy-start.17 = (bf16[1,384,512]{1,2,0:T(8,128)(2,1)S(1)}, bf16[1,384,512]{1,2,0:T(8,128)(2,1)}, u32[]{:S(2)}) copy-start(bf16[1,384,512]{1,2,0:T(8,128)(2,1)} %copy-done.16) | copy-start | bytes 1179652
  74.3 6.0 %collective-permute-start.2 = (bf16[1,128,1024]{1,2,0:T(8,128)(2,1)S(1)}, bf16[1,128,1024]{1,2,0:T(8,128)(2,1)S(1)}, u32[]{:S(2)}, u32[]{:S(2)}) collective-permute-start(bf16[1,128,1024]{1,2,0:T(8,128)(2,1)S(1)} %get-tuple-element.76), channel_id=1, source_target_pairs={{0,1},{1,2},{2,3},{3,4},{4,5},{5,6},{6,7},{7,8},{8,9},{9,10},{10,1... | collective-permute-start | bytes 786440 | tf_op jit(solution)/shard_map/ppermute | solution.py:39
  77.4 2.2 %copy-start.5 = (bf16[512,1536]{1,0:T(8,128)(2,1)S(1)}, bf16[512,1536]{1,0:T(8,128)(2,1)}, u32[]{:S(2)}) copy-start(bf16[512,1536]{1,0:T(8,128)(2,1)} %param.24) | copy-start | bytes 4718596
  77.4 5.5 %collective-permute-start.3 = (bf16[1,128,1024]{1,2,0:T(8,128)(2,1)S(1)}, bf16[1,128,1024]{1,2,0:T(8,128)(2,1)S(1)}, u32[]{:S(2)}, u32[]{:S(2)}) collective-permute-start(bf16[1,128,1024]{1,2,0:T(8,128)(2,1)S(1)} %get-tuple-element.77), channel_id=1, source_target_pairs={{1,0},{2,1},{3,2},{4,3},{5,4},{6,5},{7,6},{8,7},{9,8},{10,9},{11,1... | collective-permute-start | bytes 786440 | tf_op jit(solution)/shard_map/ppermute | solution.py:39
  80.3 3.8 %copy-start.9 = (bf16[1,128,512]{2,1,0:T(8,128)(2,1)S(1)}, bf16[1,128,512]{2,1,0:T(8,128)(2,1)}, u32[]{:S(2)}) copy-start(bf16[1,128,512]{2,1,0:T(8,128)(2,1)} %param.20) | copy-start | bytes 393220
  86.1 17.2 %copy-start.19 = (bf16[32,512]{1,0:T(8,128)(2,1)S(1)}, bf16[32,512]{1,0:T(8,128)(2,1)}, u32[]{:S(2)}) copy-start(bf16[32,512]{1,0:T(8,128)(2,1)} %copy-done.18) | copy-start | bytes 98308
  86.1 16.5 %all-to-all-start.2 = ((bf16[1,16,8,512]{3,2,0,1:T(8,128)(2,1)}), bf16[1,16,8,512]{3,2,0,1:T(8,128)(2,1)S(1)}, u32[]{:S(2)}, u32[]{:S(2)}) async-start(bf16[1,16,8,512]{3,2,0,1:T(8,128)(2,1)} %bitcast.65), calls=%async_computation.2 | async-start | bytes 262144 | tf_op jit(solution)/shard_map/all_to_all | solution.py:224
  94.7 69.9 %reduce-scatter.3.cloned.1.call-start = ((), (), s32[]{:S(2)}) async-start(), calls=%async_computation.6 | async-start | bytes 2228224 | tf_op jit(solution)/shard_map/reduce_scatter | solution.py:241
  105.1 1.0 copy-start.7
  105.1 1.6 copy-start.15
  105.1 1.6 copy-start.12
  105.1 2.0 %copy-start.23 = (bf16[32,8,64]{2,1,0:T(8,128)(2,1)S(1)}, bf16[32,8,64]{2,1,0:T(8,128)(2,1)}, u32[]{:S(2)}) copy-start(bf16[32,8,64]{2,1,0:T(8,128)(2,1)} %copy-done.22) | copy-start | bytes 98308
  105.2 2.3 %copy-start.21 = (bf16[32,8,64]{2,1,0:T(8,128)(2,1)S(1)}, bf16[32,8,64]{2,1,0:T(8,128)(2,1)}, u32[]{:S(2)}) copy-start(bf16[32,8,64]{2,1,0:T(8,128)(2,1)} %copy-done.20) | copy-start | bytes 98308
  110.2 55.9 %all-to-all-start.3 = ((bf16[1,16,8,512]{3,2,0,1:T(8,128)(2,1)}), bf16[1,16,8,512]{3,2,0,1:T(8,128)(2,1)S(1)}, u32[]{:S(2)}, u32[]{:S(2)}) async-start(bf16[1,16,8,512]{3,2,0,1:T(8,128)(2,1)} %slice_bitcast_fusion), calls=%async_computation.3 | async-start | bytes 262144 | tf_op jit(solution)/shard_map/all_to_all | solution.py:232
  113.7 62.0 %reduce-scatter.5.cloned.1.call-start = ((), (), s32[]{:S(2)}) async-start(), calls=%async_computation.7 | async-start | bytes 98304 | tf_op jit(solution)/shard_map/reduce_scatter | solution.py:242
Sparse Core Ops, SparseCore 0:
  105.3 59.2 reduce-scatter.2
  166.8 8.8 reduce-scatter.4
where the time goes:
time: 185 us; the launch traced here: 184 us
  waiting for transfers between devices  76.9 us (42%)
  starting transfers between devices  33.5 us (18%)
  local copies, waits for them, and re-layouts  27.4 us (15%)
  between operations  16.1 us (9%)
  matrix products  16 us (9%)
  other arithmetic  14 us (8%)
    reduce_scatter x1, waiting for transfers between devices, shards(): lax.psum_scatter(stacked, 'grid', scatter_dimension=1, tiled=True)  50.8 us
    all_to_all x1, starting transfers between devices, shards(): lax.all_to_all(from_tiles(dinputs.astype(jnp.bfloat16)), 'grid', split_ax...  8.59 us
    reduce_scatter x1, waiting for transfers between devices, shards(): lax.psum_scatter(partial_sum.astype(jnp.bfloat16), 'slide', scatter_dimen...  7.77 us
    all_to_all x1, starting transfers between devices, shards(): lax.all_to_all(from_tiles(embeddings), 'grid', split_axis=1, concat_axis=...  7.38 us
    gather x9, local copies, waits for them, and re-layouts, pick_rows(): source_rows[where_at]  7.37 us
    all_to_all x1, waiting for transfers between devices, shards(): lax.all_to_all(from_tiles(dinputs.astype(jnp.bfloat16)), 'grid', split_ax...  6.95 us
    all_to_all x1, waiting for transfers between devices, shards(): lax.all_to_all(shortened(to_slots(encoded)), 'grid', split_axis=1, concat...  5.41 us
    ppermute x2, starting transfers between devices, shifted(): return lax.ppermute(block, axis, route)  4.54 us
  transfers between devices with their start and end apart: 10, of which 6 were waited for; matrix products, arithmetic and copies ran while one was open for 11% of the time, Pallas kernels for 0%

commit v1 on v0

v1 whole, which is shorter than its diff:
```python
import functools
import math

import jax
import jax.numpy as jnp
from jax import lax
from jax.experimental import pallas as pl
from jax.experimental.pallas import tpu as pltpu
from jax.sharding import PartitionSpec as P

HEADS = 8
EPS = 1e-06
CAP = 8
NEG = -1e30
BF = jnp.bfloat16
F32 = jnp.float32
I32 = jnp.int32
MESH = pl.DeviceIdType.MESH


def mm(a, b):
    return lax.dot_general(a, b, (((1,), (0,)), ((), ())), preferred_element_type=F32)


def mm_nt(a, b):
    return lax.dot_general(a, b, (((1,), (1,)), ((), ())), preferred_element_type=F32)


def mm_tn(a, b):
    return lax.dot_general(a, b, (((0,), (0,)), ((), ())), preferred_element_type=F32)


def iota(shape, dim):
    return lax.broadcasted_iota(I32, shape, dim)


def norm_scale(x):
    return lax.rsqrt(jnp.mean(x * x, axis=-1, keepdims=True) + EPS)


def norm_back(x, r, dn):
    return r * dn - x * (r * r * r * jnp.mean(dn * x, axis=-1, keepdims=True))


def pack(rows, peers):
    width = rows.shape[1]
    cube = rows.reshape(peers, CAP, width)
    halves = [cube[:, :, : width // 2], cube[:, :, width // 2 :]]
    return jnp.concatenate(halves, axis=1).astype(BF)


def unpack(cube):
    peers, rows, half = cube.shape
    wide = cube.astype(F32)
    wide = jnp.concatenate([wide[:, :CAP], wide[:, CAP:]], axis=2)
    return wide.reshape(peers * CAP, 2 * half).astype(BF)


def one_hot(ids, count):
    return jnp.where(iota((ids.shape[0], count), 1) == ids, 1.0, 0.0).astype(BF)


def as_columns(row):
    n = row.shape[1]
    return jnp.broadcast_to(row, (n, n)).T


def kernel(
    groups, slides, near,
    emb, vis, win, og, mask_token, enc_qkv, enc_out, dec_qkv, dec_out,
    out_tiles, out_enc, out_dec,
    sbuf, rbuf, og_halo, h_send, h_halo,
    dec_a_send, dec_b_send, dec_a, dec_b,
    enc_a_send, enc_b_send, enc_a, enc_b,
    far_send, far_recv, far_own, acc,
    a2a_ss, a2a_rs, halo_ss, halo_rs, near_ss, near_rs, far_ss, far_rs,
):
    s = lax.axis_index("slide")
    g = lax.axis_index("grid")
    tiles, width = emb.shape[1:]
    vis_all = vis.shape[1]
    tokens = vis_all // groups
    far = groups // near
    rb, cw = out_enc.shape
    n = lax.rem(g, near)
    f = lax.div(g, near)
    log_g = groups.bit_length() - 1
    pending = []

    barrier = pltpu.get_barrier_semaphore()
    met = 0
    for j in range(1, groups):
        pl.semaphore_signal(
            barrier, inc=1, device_id=(s, lax.rem(g + j, groups)), device_id_type=MESH
        )
        met += 1
    for ds in range(1, slides):
        for dn in range(near):
            peer = (lax.rem(s + ds, slides), f * near + lax.rem(n + dn, near))
            pl.semaphore_signal(barrier, inc=1, device_id=peer, device_id_type=MESH)
            met += 1

    def send(src, dst, ss, rs, peer):
        copy = pltpu.make_async_remote_copy(
            src_ref=src, dst_ref=dst, send_sem=ss, recv_sem=rs,
            device_id=peer, device_id_type=MESH,
        )
        copy.start()
        return copy

    def all_to_all_start(stage):
        copies = []
        for j in range(1, groups):
            dst = lax.rem(g + j, groups)
            copies.append(
                send(sbuf.at[stage, dst], rbuf.at[stage, g], a2a_ss.at[stage, j],
                     a2a_rs.at[stage, j], (s, dst))
            )
        rbuf[stage, g] = sbuf[stage, g]
        pending.extend(copies)
        return copies

    def all_to_all_wait(stage):
        for j in range(1, groups):
            src = lax.rem(g + groups - j, groups)
            pltpu.make_async_remote_copy(
                src_ref=sbuf.at[stage, src], dst_ref=rbuf.at[stage, src],
                send_sem=a2a_ss.at[stage, j], recv_sem=a2a_rs.at[stage, j],
                device_id=(s, src), device_id_type=MESH,
            ).wait_recv()
        return unpack(rbuf[stage])

    def halo_copies(kind, src, dst):
        left = jnp.maximum(g - 1, 0)
        right = jnp.minimum(g + 1, groups - 1)

        def to(side, peer):
            return pltpu.make_async_remote_copy(
                src_ref=src, dst_ref=dst.at[side], send_sem=halo_ss.at[kind, side],
                recv_sem=halo_rs.at[kind, side], device_id=(s, peer), device_id_type=MESH,
            )

        return to(1, left), to(0, right)

    def halo_start(kind, src, dst):
        to_left, to_right = halo_copies(kind, src, dst)

        @pl.when(g > 0)
        def _():
            to_left.start()

        @pl.when(g < groups - 1)
        def _():
            to_right.start()

    def halo_wait(kind, src, dst):
        to_left, to_right = halo_copies(kind, src, dst)

        @pl.when(g > 0)
        def _():
            to_right.wait_recv()

        @pl.when(g == 0)
        def _():
            dst[0] = jnp.zeros(dst.shape[1:], dst.dtype)

        @pl.when(g < groups - 1)
        def _():
            to_left.wait_recv()

        @pl.when(g == groups - 1)
        def _():
            dst[1] = jnp.zeros(dst.shape[1:], dst.dtype)

    def halo_end(kind, src, dst):
        to_left, to_right = halo_copies(kind, src, dst)

        @pl.when(g > 0)
        def _():
            to_left.wait_send()

        @pl.when(g < groups - 1)
        def _():
            to_right.wait_send()

    def near_start(kind, src, dst, by_slide):
        copies = []
        for ds in range(slides):
            for dn in range(near):
                o = ds * near + dn
                s2, n2 = lax.rem(s + ds, slides), lax.rem(n + dn, near)
                part = src.at[s2] if by_slide else src.at[n2]
                if o == 0:
                    dst[0] = part[...]
                else:
                    copies.append(
                        send(part, dst.at[o], near_ss.at[kind, o], near_rs.at[kind, o],
                             (s2, f * near + n2))
                    )
        pending.extend(copies)
        return copies

    def far_start(which, part):
        cube = part.reshape(far, rb, cw)
        far_own[...] = cube
        far_send[which] = cube.astype(far_send.dtype)
        copies = []
        for df in range(1, far):
            f2 = lax.rem(f + df, far)
            copies.append(
                send(far_send.at[which, f2], far_recv.at[which, df], far_ss.at[which, df],
                     far_rs.at[which, df], (s, f2 * near + n))
            )
        pending.extend(copies)
        return far_own[f], copies

    def far_end(own, copies, which):
        total = own
        for df, copy in enumerate(copies, 1):
            copy.wait_recv()
            total = total + far_recv[which, df].astype(F32)
        return total

    def near_product(a, b):
        return mm_tn(a[...].reshape(-1, a.shape[2]), b[...].reshape(-1, b.shape[2]))

    vis_row = vis[...]
    t_col = g * tiles + iota((tiles, 1), 0)

    def is_visible(ids):
        return jnp.sum(jnp.where(vis_row == ids, 1.0, 0.0), axis=1, keepdims=True)

    rank = jnp.sum(jnp.where(vis_row < t_col, 1.0, 0.0), axis=1, keepdims=True).astype(I32)
    here = is_visible(t_col)
    slot = jnp.bitwise_and(rank, groups - 1) * CAP + jnp.bitwise_and(
        jnp.right_shift(rank, log_g), CAP - 1
    )
    by_tile = one_hot(jnp.where(here > 0.5, slot, -1), groups * CAP)
    sbuf[0] = pack(mm_tn(by_tile, emb[0]), groups)

    pl.semaphore_wait(barrier, met)
    first = all_to_all_start(0)
    halo_start(0, og.at[0], og_halo)

    rank_row = iota((tokens, vis_all), 1)
    mine = rank_row == iota((tokens, vis_all), 0) * groups + g
    token_tile = jnp.sum(
        jnp.where(mine, vis_row.astype(F32), 0.0), axis=1, keepdims=True
    ).astype(I32)
    source = jnp.right_shift(token_tile, tiles.bit_length() - 1)
    by_token = one_hot(
        source * CAP + jnp.bitwise_and(iota((tokens, 1), 0), CAP - 1), groups * CAP
    )
    grad_out = og[0]
    for k in range(slides):
        dec_b_send[k] = grad_out[:, k * cw : (k + 1) * cw]
    dctx_mid = mm_nt(grad_out, dec_out[...]).astype(BF)
    new = iota((1, width), 1)
    span = far * rb
    low = jnp.bitwise_and(new, span - 1)
    old = (
        jnp.right_shift(low, rb.bit_length() - 1) * near
        + jnp.right_shift(new, span.bit_length() - 1)
    ) * rb + jnp.bitwise_and(low, rb - 1)
    shuffle = jnp.where(iota((width, width), 0) == old, 1.0, 0.0).astype(BF)

    def near_columns(values, dst):
        moved = mm(values, shuffle).astype(BF)
        for k in range(near):
            dst[k] = moved[:, k * span : (k + 1) * span]

    slots = all_to_all_wait(0)
    dec_b_copies = near_start(0, dec_b_send, dec_b, True)

    tok = mm(by_token, slots)
    tok_r = norm_scale(tok)
    proj = mm((tok * tok_r).astype(BF), enc_qkv[...]).astype(BF)
    q, k, v = proj[:, :width], proj[:, width : 2 * width], proj[:, 2 * width :]
    head_width = width // HEADS
    scale = 1.0 / math.sqrt(head_width)
    rows = HEADS * tokens
    heads = jnp.where(
        jnp.right_shift(iota((rows, width), 0), tokens.bit_length() - 1)
        == jnp.right_shift(iota((rows, width), 1), head_width.bit_length() - 1),
        1.0, 0.0,
    )
    heads_b = heads.astype(BF)

    def spread(values):
        return jnp.concatenate([values] * HEADS, axis=0) * heads_b

    def gather_heads(values):
        return jnp.sum((values * heads).reshape(HEADS, tokens, width), axis=0)

    qx = spread(q)
    logits = mm_nt(qx, k) * scale
    weights = jnp.exp(logits - jnp.max(logits, axis=-1, keepdims=True))
    enc_p = weights / jnp.sum(weights, axis=-1, keepdims=True)
    enc_pb = enc_p.astype(BF)
    enc_ctx = gather_heads(mm(enc_pb, v)).astype(BF)
    encoded = (tok + mm(enc_ctx, enc_out[...])).astype(BF)
    sbuf[1] = pack(mm_tn(by_token, encoded), groups)
    all_to_all_start(1)

    w_mid = win[:, pl.ds(pl.multiple_of(g * tiles, tiles), tiles)]
    w_low = win[:, pl.ds(pl.multiple_of(jnp.maximum(g - 1, 0) * tiles, tiles), tiles)]
    w_high = win[:, pl.ds(pl.multiple_of(jnp.minimum(g + 1, groups - 1) * tiles, tiles), tiles)]
    w_low = jnp.where(g > 0, w_low, -2)
    w_high = jnp.where(g < groups - 1, w_high, -2)
    first_w, last_w = w_mid[:, :1], w_mid[:, tiles - 1 :]
    w_a = jnp.where((w_mid == first_w) | (w_low == first_w), first_w, -1)
    w_b = jnp.where((w_mid == last_w) | (w_high == last_w), last_w, -1)
    mid_columns = as_columns(w_mid)
    in_a = mid_columns[:, :1] == first_w
    in_b = mid_columns[:, :1] == last_w
    vis_low = is_visible(t_col - tiles)
    vis_high = is_visible(t_col + tiles)
    blank = mask_token[...]
    enc_ctx_cols = near_columns(enc_ctx, enc_a_send)
    halo_wait(0, og.at[0], og_halo)
    dctx_low = mm_nt(og_halo[0], dec_out[...])
    dctx_high = mm_nt(og_halo[1], dec_out[...])
    dctx_a = jnp.where(in_a, dctx_mid.astype(F32), dctx_low).astype(BF)
    dctx_b = jnp.where(in_b, dctx_mid.astype(F32), dctx_high).astype(BF)
    lane = iota((1, 2 * head_width), 1)
    half0 = jnp.where(lane < head_width, 1.0, 0.0).astype(BF)
    half1 = jnp.where(lane < head_width, 0.0, 1.0).astype(BF)
    low_half = iota((tiles, 2 * head_width), 1) < head_width

    def same_window(row):
        same = jnp.where(as_columns(row) == row, 1.0, 0.0)
        return jnp.concatenate([same, same], axis=0) > 0.5

    def window_block(qkv, dctx, row, keep):
        allowed = same_window(row)
        for pair in range(HEADS // 2):
            at = slice(pair * 2 * head_width, (pair + 1) * 2 * head_width)
            qs, ks, vs = qkv[0][:, at], qkv[1][:, at], qkv[2][:, at]
            do = dctx[:, at]
            qx = jnp.concatenate([qs * half0, qs * half1], axis=0)
            dox = jnp.concatenate([do * half0, do * half1], axis=0)
            scores = jnp.where(allowed, mm_nt(qx, ks) * scale, NEG)
            e = jnp.exp(scores - jnp.max(scores, axis=-1, keepdims=True))
            p = e / jnp.sum(e, axis=-1, keepdims=True)
            pb = p.astype(BF)
            dp = mm_nt(dox, vs).astype(BF).astype(F32)
            dsb = (p * (dp - jnp.sum(p * dp, axis=-1, keepdims=True)) * scale).astype(BF)
            o = mm(pb, vs)
            dq = mm(dsb, ks)
            results = (
                jnp.where(low_half, dq[:tiles], dq[tiles:]),
                mm_tn(dsb, qx),
                mm_tn(pb, dox),
                jnp.where(low_half, o[:tiles], o[tiles:]),
            )
            for i, value in enumerate(results):
                cols = slice(i * width + at.start, i * width + at.stop)
                if keep is not None:
                    value = jnp.where(keep, value, acc[:, cols])
                acc[:, cols] = value

    def dec_project(values, shown):
        x = jnp.where(shown > 0.5, values.astype(F32), blank)
        r = norm_scale(x)
        out = mm((x * r).astype(BF), dec_qkv[...])
        return x, r, out

    def split3(values):
        values = values.astype(BF)
        return values[:, :width], values[:, width : 2 * width], values[:, 2 * width :]

    slots = all_to_all_wait(1)
    placed = mm(by_tile, slots).astype(BF)
    h_send[...] = placed
    halo_start(1, h_send, h_halo)
    x_mid, r_mid, qkv_mid = dec_project(placed, here)
    window_block(split3(qkv_mid), dctx_mid, w_mid, None)
    halo_wait(1, h_send, h_halo)
    _, _, qkv_low = dec_project(h_halo[0], vis_low)
    window_block(split3(jnp.where(in_a, qkv_mid, qkv_low)), dctx_a, w_a, in_a)
    _, _, qkv_high = dec_project(h_halo[1], vis_high)
    window_block(split3(jnp.where(in_b, qkv_mid, qkv_high)), dctx_b, w_b, in_b)

    near_columns(acc[:, 3 * width :].astype(BF), dec_a_send)
    dec_a_copies = near_start(1, dec_a_send, dec_a, False)
    dnormed = mm_nt(acc[:, : 3 * width].astype(BF), dec_qkv[...])
    dinputs = norm_back(x_mid, r_mid, dnormed) + grad_out.astype(F32)
    sbuf[2] = pack(mm_tn(by_tile, dinputs.astype(BF)), groups)
    all_to_all_start(2)

    for copy in dec_a_copies + dec_b_copies:
        copy.wait_recv()
    dec_own, dec_far = far_start(0, near_product(dec_a, dec_b))

    grad_enc = mm(by_token, all_to_all_wait(2))
    grad_enc_b = grad_enc.astype(BF)
    for j in range(slides):
        enc_b_send[j] = grad_enc_b[:, j * cw : (j + 1) * cw]
    enc_copies = near_start(2, enc_a_send, enc_a, False) + near_start(3, enc_b_send, enc_b, True)
    dox = spread(mm_nt(grad_enc_b, enc_out[...]).astype(BF))
    dp = mm_nt(dox, v).astype(BF).astype(F32)
    dsb = (enc_p * (dp - jnp.sum(enc_p * dp, axis=-1, keepdims=True)) * scale).astype(BF)
    dq = gather_heads(mm(dsb, k))
    dk = mm_tn(dsb, qx)
    dv = mm_tn(enc_pb, dox)
    dproj = jnp.concatenate([dq, dk, dv], axis=1).astype(BF)
    dn = mm_nt(dproj, enc_qkv[...]).astype(BF).astype(F32)
    dtok = (norm_back(tok, tok_r, dn) + grad_enc).astype(BF)
    sbuf[3] = pack(mm_tn(by_token, dtok), groups)
    all_to_all_start(3)

    out_dec[...] = far_end(dec_own, dec_far, 0)
    for copy in enc_copies:
        copy.wait_recv()
    enc_own, enc_far = far_start(1, near_product(enc_a, enc_b))
    out_tiles[0] = mm(by_tile, all_to_all_wait(3)).astype(BF)
    out_enc[...] = far_end(enc_own, enc_far, 1)
    for copy in pending:
        copy.wait_send()
    halo_end(0, og.at[0], og_halo)
    halo_end(1, h_send, h_halo)


def shards(groups, slides, emb, vis, win, og, mask_token, enc_qkv, enc_out, dec_qkv, dec_out):
    _, tiles, width = emb.shape
    tokens = vis.shape[1] // groups
    near = min(4, groups)
    far = groups // near
    rb, cw = width // groups, width // slides
    span = far * rb
    ns = near * slides
    far_type = BF if rb % 16 == 0 else F32
    dma = pltpu.SemaphoreType.DMA
    vmem = pl.BlockSpec(memory_space=pltpu.VMEM)
    return pl.pallas_call(
        functools.partial(kernel, groups, slides, near),
        out_shape=(
            jax.ShapeDtypeStruct(emb.shape, BF),
            jax.ShapeDtypeStruct((rb, cw), F32),
            jax.ShapeDtypeStruct((rb, cw), F32),
        ),
        in_specs=[vmem] * 9,
        out_specs=(vmem,) * 3,
        scratch_shapes=[
            pltpu.VMEM((4, groups, 2 * CAP, width // 2), BF),
            pltpu.VMEM((4, groups, 2 * CAP, width // 2), BF),
            pltpu.VMEM((2, tiles, width), BF),
            pltpu.VMEM((tiles, width), BF),
            pltpu.VMEM((2, tiles, width), BF),
            pltpu.VMEM((near, tiles, span), BF),
            pltpu.VMEM((slides, tiles, cw), BF),
            pltpu.VMEM((ns, tiles, span), BF),
            pltpu.VMEM((ns, tiles, cw), BF),
            pltpu.VMEM((near, tokens, span), BF),
            pltpu.VMEM((slides, tokens, cw), BF),
            pltpu.VMEM((ns, tokens, span), BF),
            pltpu.VMEM((ns, tokens, cw), BF),
            pltpu.VMEM((2, far, rb, cw), far_type),
            pltpu.VMEM((2, far, rb, cw), far_type),
            pltpu.VMEM((far, rb, cw), F32),
            pltpu.VMEM((tiles, 4 * width), F32),
            dma((4, groups)), dma((4, groups)),
            dma((2, 2)), dma((2, 2)),
            dma((4, ns)), dma((4, ns)),
            dma((2, far)), dma((2, far)),
        ],
        compiler_params=pltpu.CompilerParams(
            collective_id=0, has_side_effects=True, vmem_limit_bytes=44 * 1024 * 1024
        ),
    )(emb, vis, win, og, mask_token[None, :], enc_qkv, enc_out, dec_qkv, dec_out)


def solution(mesh):
    placed = (
        P("slide", "grid", None),
        P("slide", None),
        P("slide", None),
        P("slide", "grid", None),
        P(),
        P(),
        P(),
        P(),
        P(),
    )
    return jax.shard_map(
        functools.partial(shards, mesh.shape["grid"], mesh.shape["slide"]),
        mesh=mesh,
        in_specs=placed,
        out_specs=(P("slide", "grid", None), P("grid", "slide"), P("grid", "slide")),
        check_vma=False,
    )
```

time: 185 us -> 57.2 us (0.31)
  waiting for transfers between devices: 76.9 us -> 0 us
  Pallas kernels: 0 us -> 45.6 us
  starting transfers between devices: 33.5 us -> 0 us
  local copies, waits for them, and re-layouts: 27.4 us -> 10.6 us
  matrix products: 16 us -> 0 us
  between operations: 16.1 us -> 0.66 us
  other arithmetic: 14 us -> 0 us
    reduce_scatter x2 -> x0, waiting for transfers between devices: 58.5 us -> none  [the longest x1 50.8 us: shards(): lax.psum_scatter(stacked, 'grid', scatter_dimension=1, tiled=True)]
    pallas_call x0 -> x1, Pallas kernels: none -> 45.6 us  [shards(): pl.pallas_call(functools.partial(kernel, groups, slides, near), out_shape...]
    all_to_all x4 -> x0, starting transfers between devices: 23.7 us -> none  [the longest x1 8.59 us: shards(): lax.all_to_all(from_tiles(dinputs.astype(jnp.bfloat16)), 'grid', split_ax...]
    all_to_all x4 -> x0, waiting for transfers between devices: 15.7 us -> none  [the longest x1 6.95 us: shards(): lax.all_to_all(from_tiles(dinputs.astype(jnp.bfloat16)), 'grid', split_ax...]
    dot_general x21 -> x0, matrix products: 13.2 us -> none  [the longest x6 2.55 us: attend(): jnp.einsum('...wvy,...ywj->...vwj', attention_probs, value_per_head)]
    gather x11 -> x0, local copies, waits for them, and re-layouts: 10.6 us -> none  [the longest x9 7.37 us: pick_rows(): source_rows[where_at]]
    ppermute x4 -> x0, starting transfers between devices: 9.55 us -> none  [the longest x2 4.54 us: shifted(): return lax.ppermute(block, axis, route)]
    unnamed x56 -> x21, local copies, waits for them, and re-layouts: 2.7 us -> 10.6 us
  transfers between devices with their start and end apart: 10 -> 0, of which waited for: 6 -> 0; matrix products, arithmetic and copies ran while one was open for 11% -> 0% of each run, Pallas kernels for 0% -> 0%
where the time goes in v1:
time: 57.2 us; the launch traced here: 56.9 us
  Pallas kernels  45.6 us (80%)
  local copies, waits for them, and re-layouts  10.6 us (19%)
  between operations  0.66 us (1%)
    pallas_call x1, Pallas kernels, shards(): pl.pallas_call(functools.partial(kernel, groups, slides, near), out_shape...  45.6 us
    unnamed x21, local copies, waits for them, and re-layouts  10.6 us

profile of v1, /device:TPU:0, one launch (start us, length us, event | category | flops | bytes accessed | tf_op | source)
XLA Modules:
  0.0 56.9 jit_solution(2714819958003361517)
XLA Ops:
  0.6 0.0 copy-start
  0.6 1.4 %copy-done = bf16[512,1536]{1,0:T(8,128)(2,1)S(1)} copy-done((bf16[512,1536]{1,0:T(8,128)(2,1)S(1)}, bf16[512,1536]{1,0:T(8,128)(2,1)}, u32[]{:S(2)}) %copy-start) | copy-done | bytes 1572888
  2.0 0.0 copy-start.1
  2.0 1.4 %copy-done.1 = bf16[512,1536]{1,0:T(8,128)(2,1)S(1)} copy-done((bf16[512,1536]{1,0:T(8,128)(2,1)S(1)}, bf16[512,1536]{1,0:T(8,128)(2,1)}, u32[]{:S(2)}) %copy-start.1) | copy-done | bytes 1572888
  3.5 0.0 copy-start.2
  3.5 1.0 %copy-done.2 = bf16[512,512]{1,0:T(8,128)(2,1)S(1)} copy-done((bf16[512,512]{1,0:T(8,128)(2,1)S(1)}, bf16[512,512]{1,0:T(8,128)(2,1)}, u32[]{:S(2)}) %copy-start.2) | copy-done | bytes 524312
  4.5 0.0 copy-start.3
  4.5 1.0 %copy-done.3 = bf16[512,512]{1,0:T(8,128)(2,1)S(1)} copy-done((bf16[512,512]{1,0:T(8,128)(2,1)S(1)}, bf16[512,512]{1,0:T(8,128)(2,1)}, u32[]{:S(2)}) %copy-start.3) | copy-done | bytes 524312
  5.5 0.0 copy-start.4
  5.5 0.9 %copy-done.4 = bf16[1,128,512]{2,1,0:T(8,128)(2,1)S(1)} copy-done((bf16[1,128,512]{2,1,0:T(8,128)(2,1)S(1)}, bf16[1,128,512]{2,1,0:T(8,128)(2,1)}, u32[]{:S(2)}) %copy-start.4) | copy-done | bytes 131096
  6.4 0.0 copy-start.5
  6.4 0.9 %copy-done.5 = bf16[1,128,512]{2,1,0:T(8,128)(2,1)S(1)} copy-done((bf16[1,128,512]{2,1,0:T(8,128)(2,1)S(1)}, bf16[1,128,512]{2,1,0:T(8,128)(2,1)}, u32[]{:S(2)}) %copy-start.5) | copy-done | bytes 131096
  7.3 0.0 copy-start.6
  7.3 0.7 %copy-done.6 = s32[1,2048]{1,0:T(1,128)S(1)} copy-done((s32[1,2048]{1,0:T(1,128)S(1)}, s32[1,2048]{1,0:T(1,128)}, u32[]{:S(2)}) %copy-start.6) | copy-done | bytes 8216
  8.0 0.0 copy-start.7
  8.0 0.7 %copy-done.7 = s32[1,512]{1,0:T(1,128)S(1)} copy-done((s32[1,512]{1,0:T(1,128)S(1)}, s32[1,512]{1,0:T(1,128)}, u32[]{:S(2)}) %copy-start.7) | copy-done | bytes 2072
  8.7 0.0 copy-start.8
  8.7 0.7 %copy-done.8 = f32[512]{0:T(512)S(1)} copy-done((f32[512]{0:T(512)S(1)}, f32[512]{0:T(512)}, u32[]{:S(2)}) %copy-start.8) | copy-done | bytes 2072
  9.4 45.6 %shard_map.112 = (bf16[1,128,512]{2,1,0:T(8,128)(2,1)S(1)}, f32[32,256]{1,0:T(8,128)S(1)}, f32[32,256]{1,0:T(8,128)S(1)}) custom-call(bf16[1,128,512]{2,1,0:T(8,128)(2,1)S(1)} %copy-done.4, s32[1,512]{1,0:T(1,128)S(1)} %copy-done.7, s32[1,2048]{1,0:T(1,128)S(1)} %copy-done.6, bf16[1,128,512]{2,1,0:T(8,128)(2,1)S(1)} %copy-done.5, f32[1,512]{1,0:T(1,128)S(1)} %bitcast.1, ...), custom_call_target="tpu_custom_call" | custom-call | tf_op jit(solution)/shard_map/pallas_call | solution.py:435
  55.0 0.7 %copy.15 = bf16[1,128,512]{2,1,0:T(8,128)(2,1)} copy(bf16[1,128,512]{2,1,0:T(8,128)(2,1)S(1)} %get-tuple-element.6) | data formatting | bytes 262144
  55.6 0.6 %copy.16 = f32[32,256]{1,0:T(8,128)} copy(f32[32,256]{1,0:T(8,128)S(1)} %get-tuple-element.7) | data formatting | bytes 65536
  56.2 0.6 %copy.17 = f32[32,256]{1,0:T(8,128)} copy(f32[32,256]{1,0:T(8,128)S(1)} %get-tuple-element.8) | data formatting | bytes 65536
Async XLA Ops:
  0.6 1.4 %copy-start = (bf16[512,1536]{1,0:T(8,128)(2,1)S(1)}, bf16[512,1536]{1,0:T(8,128)(2,1)}, u32[]{:S(2)}) copy-start(bf16[512,1536]{1,0:T(8,128)(2,1)} %enc_qkv.1) | copy-start | bytes 4718596
  2.0 1.4 %copy-start.1 = (bf16[512,1536]{1,0:T(8,128)(2,1)S(1)}, bf16[512,1536]{1,0:T(8,128)(2,1)}, u32[]{:S(2)}) copy-start(bf16[512,1536]{1,0:T(8,128)(2,1)} %dec_qkv.1) | copy-start | bytes 4718596
  3.5 1.0 %copy-start.2 = (bf16[512,512]{1,0:T(8,128)(2,1)S(1)}, bf16[512,512]{1,0:T(8,128)(2,1)}, u32[]{:S(2)}) copy-start(bf16[512,512]{1,0:T(8,128)(2,1)} %enc_out.1) | copy-start | bytes 1572868
  4.5 1.0 %copy-start.3 = (bf16[512,512]{1,0:T(8,128)(2,1)S(1)}, bf16[512,512]{1,0:T(8,128)(2,1)}, u32[]{:S(2)}) copy-start(bf16[512,512]{1,0:T(8,128)(2,1)} %dec_out.1) | copy-start | bytes 1572868
  5.5 0.9 %copy-start.4 = (bf16[1,128,512]{2,1,0:T(8,128)(2,1)S(1)}, bf16[1,128,512]{2,1,0:T(8,128)(2,1)}, u32[]{:S(2)}) copy-start(bf16[1,128,512]{2,1,0:T(8,128)(2,1)} %emb.1) | copy-start | bytes 393220
  6.4 0.9 %copy-start.5 = (bf16[1,128,512]{2,1,0:T(8,128)(2,1)S(1)}, bf16[1,128,512]{2,1,0:T(8,128)(2,1)}, u32[]{:S(2)}) copy-start(bf16[1,128,512]{2,1,0:T(8,128)(2,1)} %og.1) | copy-start | bytes 393220
  7.3 0.7 %copy-start.6 = (s32[1,2048]{1,0:T(1,128)S(1)}, s32[1,2048]{1,0:T(1,128)}, u32[]{:S(2)}) copy-start(s32[1,2048]{1,0:T(1,128)} %win.1) | copy-start | bytes 24580
  8.0 0.7 %copy-start.7 = (s32[1,512]{1,0:T(1,128)S(1)}, s32[1,512]{1,0:T(1,128)}, u32[]{:S(2)}) copy-start(s32[1,512]{1,0:T(1,128)} %vis.1) | copy-start | bytes 6148
  8.7 0.7 %copy-start.8 = (f32[512]{0:T(512)S(1)}, f32[512]{0:T(512)}, u32[]{:S(2)}) copy-start(f32[512]{0:T(512)} %param.13) | copy-start | bytes 6148

commit v2 on v1

--- a/solution.py
+++ b/solution.py
@@ -67,17 +67,18 @@
 
 def kernel(
     groups, slides, near,
+    emb_in, vis_in, win_in, og_in, mask_in, enc_qkv_in, enc_out_in, dec_qkv_in, dec_out_in,
+    out_tiles, out_enc, out_dec,
     emb, vis, win, og, mask_token, enc_qkv, enc_out, dec_qkv, dec_out,
-    out_tiles, out_enc, out_dec,
     sbuf, rbuf, og_halo, h_send, h_halo,
     dec_a_send, dec_b_send, dec_a, dec_b,
     enc_a_send, enc_b_send, enc_a, enc_b,
-    far_send, far_recv, far_own, acc,
+    far_send, far_recv, far_own, acc_q, acc_kv, acc_o, load_s,
     a2a_ss, a2a_rs, halo_ss, halo_rs, near_ss, near_rs, far_ss, far_rs,
 ):
     s = lax.axis_index("slide")
     g = lax.axis_index("grid")
-    tiles, width = emb.shape[1:]
+    tiles, width = emb.shape
     vis_all = vis.shape[1]
     tokens = vis_all // groups
     far = groups // near
@@ -86,6 +87,19 @@
     f = lax.div(g, near)
     log_g = groups.bit_length() - 1
     pending = []
+    loads = []
+    for i, (src, dst) in enumerate((
+        (vis_in, vis), (emb_in.at[0], emb), (og_in.at[0], og), (enc_qkv_in, enc_qkv),
+        (dec_out_in, dec_out), (win_in, win), (enc_out_in, enc_out), (mask_in, mask_token),
+        (dec_qkv_in, dec_qkv),
+    )):
+        loads.append((dst, pltpu.make_async_copy(src, dst, load_s.at[i])))
+        loads[i][1].start()
+
+    def loaded(*refs):
+        for dst, copy in loads:
+            if any(dst is ref for ref in refs):
+                copy.wait()
 
     barrier = pltpu.get_barrier_semaphore()
     met = 0
@@ -110,7 +124,7 @@
 
     def all_to_all_start(stage):
         copies = []
-        for j in range(1, groups):
+        for j in sorted(range(1, groups), key=lambda j: -min(j, groups - j)):
             dst = lax.rem(g + j, groups)
             copies.append(
                 send(sbuf.at[stage, dst], rbuf.at[stage, g], a2a_ss.at[stage, j],
@@ -224,6 +238,7 @@
     def near_product(a, b):
         return mm_tn(a[...].reshape(-1, a.shape[2]), b[...].reshape(-1, b.shape[2]))
 
+    loaded(vis)
     vis_row = vis[...]
     t_col = g * tiles + iota((tiles, 1), 0)
 
@@ -236,11 +251,13 @@
         jnp.right_shift(rank, log_g), CAP - 1
     )
     by_tile = one_hot(jnp.where(here > 0.5, slot, -1), groups * CAP)
-    sbuf[0] = pack(mm_tn(by_tile, emb[0]), groups)
+    loaded(emb)
+    sbuf[0] = pack(mm_tn(by_tile, emb[...]), groups)
 
     pl.semaphore_wait(barrier, met)
-    first = all_to_all_start(0)
-    halo_start(0, og.at[0], og_halo)
+    all_to_all_start(0)
+    loaded(og)
+    halo_start(0, og, og_halo)
 
     rank_row = iota((tokens, vis_all), 1)
     mine = rank_row == iota((tokens, vis_all), 0) * groups + g
@@ -251,9 +268,10 @@
     by_token = one_hot(
         source * CAP + jnp.bitwise_and(iota((tokens, 1), 0), CAP - 1), groups * CAP
     )
-    grad_out = og[0]
+    grad_out = og[...]
     for k in range(slides):
         dec_b_send[k] = grad_out[:, k * cw : (k + 1) * cw]
+    loaded(dec_out)
     dctx_mid = mm_nt(grad_out, dec_out[...]).astype(BF)
     new = iota((1, width), 1)
     span = far * rb
@@ -264,13 +282,13 @@
     ) * rb + jnp.bitwise_and(low, rb - 1)
     shuffle = jnp.where(iota((width, width), 0) == old, 1.0, 0.0).astype(BF)
 
-    def near_columns(values, dst):
-        moved = mm(values, shuffle).astype(BF)
+    def near_columns(values, dst, product=mm):
+        moved = product(values, shuffle).astype(BF)
         for k in range(near):
             dst[k] = moved[:, k * span : (k + 1) * span]
 
+    loaded(enc_qkv, enc_out, win, mask_token, dec_qkv)
     slots = all_to_all_wait(0)
-    dec_b_copies = near_start(0, dec_b_send, dec_b, True)
 
     tok = mm(by_token, slots)
     tok_r = norm_scale(tok)
@@ -293,11 +311,11 @@
         return jnp.sum((values * heads).reshape(HEADS, tokens, width), axis=0)
 
     qx = spread(q)
-    logits = mm_nt(qx, k) * scale
-    weights = jnp.exp(logits - jnp.max(logits, axis=-1, keepdims=True))
-    enc_p = weights / jnp.sum(weights, axis=-1, keepdims=True)
+    logits = mm_nt(k, qx) * scale
+    weights = jnp.exp(logits - jnp.max(logits, axis=0, keepdims=True))
+    enc_p = weights / jnp.sum(weights, axis=0, keepdims=True)
     enc_pb = enc_p.astype(BF)
-    enc_ctx = gather_heads(mm(enc_pb, v)).astype(BF)
+    enc_ctx = gather_heads(mm_tn(enc_pb, v)).astype(BF)
     encoded = (tok + mm(enc_ctx, enc_out[...])).astype(BF)
     sbuf[1] = pack(mm_tn(by_token, encoded), groups)
     all_to_all_start(1)
@@ -316,8 +334,8 @@
     vis_low = is_visible(t_col - tiles)
     vis_high = is_visible(t_col + tiles)
     blank = mask_token[...]
-    enc_ctx_cols = near_columns(enc_ctx, enc_a_send)
-    halo_wait(0, og.at[0], og_halo)
+    near_columns(enc_ctx, enc_a_send)
+    halo_wait(0, og, og_halo)
     dctx_low = mm_nt(og_halo[0], dec_out[...])
     dctx_high = mm_nt(og_halo[1], dec_out[...])
     dctx_a = jnp.where(in_a, dctx_mid.astype(F32), dctx_low).astype(BF)
@@ -325,39 +343,46 @@
     lane = iota((1, 2 * head_width), 1)
     half0 = jnp.where(lane < head_width, 1.0, 0.0).astype(BF)
     half1 = jnp.where(lane < head_width, 0.0, 1.0).astype(BF)
-    low_half = iota((tiles, 2 * head_width), 1) < head_width
+    scaled0, scaled1 = half0 * BF(scale), half1 * BF(scale)
+    at_a, at_b = w_mid == first_w, w_mid == last_w
 
     def same_window(row):
-        same = jnp.where(as_columns(row) == row, 1.0, 0.0)
-        return jnp.concatenate([same, same], axis=0) > 0.5
-
-    def window_block(qkv, dctx, row, keep):
-        allowed = same_window(row)
+        same = jnp.where(as_columns(row) == row, 0.0, NEG)
+        return jnp.concatenate([same, same], axis=1)
+
+    def diagonal(values):
+        return jnp.concatenate(
+            [values[:head_width, :tiles], values[head_width:, tiles:]], axis=0
+        )
+
+    def window_block(qkv, dctx, row, keep_rows, keep_lanes):
+        bias = same_window(row)
         for pair in range(HEADS // 2):
             at = slice(pair * 2 * head_width, (pair + 1) * 2 * head_width)
             qs, ks, vs = qkv[0][:, at], qkv[1][:, at], qkv[2][:, at]
             do = dctx[:, at]
-            qx = jnp.concatenate([qs * half0, qs * half1], axis=0)
+            qx = jnp.concatenate([qs * scaled0, qs * scaled1], axis=0)
             dox = jnp.concatenate([do * half0, do * half1], axis=0)
-            scores = jnp.where(allowed, mm_nt(qx, ks) * scale, NEG)
-            e = jnp.exp(scores - jnp.max(scores, axis=-1, keepdims=True))
-            p = e / jnp.sum(e, axis=-1, keepdims=True)
+            scores = mm_nt(ks, qx) + bias
+            e = jnp.exp(scores - jnp.max(scores, axis=0, keepdims=True))
+            p = e * (1.0 / jnp.sum(e, axis=0, keepdims=True))
             pb = p.astype(BF)
-            dp = mm_nt(dox, vs).astype(BF).astype(F32)
-            dsb = (p * (dp - jnp.sum(p * dp, axis=-1, keepdims=True)) * scale).astype(BF)
-            o = mm(pb, vs)
-            dq = mm(dsb, ks)
-            results = (
-                jnp.where(low_half, dq[:tiles], dq[tiles:]),
-                mm_tn(dsb, qx),
-                mm_tn(pb, dox),
-                jnp.where(low_half, o[:tiles], o[tiles:]),
-            )
-            for i, value in enumerate(results):
-                cols = slice(i * width + at.start, i * width + at.stop)
-                if keep is not None:
-                    value = jnp.where(keep, value, acc[:, cols])
-                acc[:, cols] = value
+            dp = mm_nt(vs, dox)
+            dsb = (p * (dp - jnp.sum(p * dp, axis=0, keepdims=True))).astype(BF)
+            o = diagonal(mm_tn(vs, pb))
+            dq = diagonal(mm_tn(ks, dsb))
+            dk = mm(dsb, qx)
+            dv = mm(pb, dox)
+            at_v = slice(width + at.start, width + at.stop)
+            if keep_rows is not None:
+                o = jnp.where(keep_lanes, o, acc_o[at])
+                dq = jnp.where(keep_lanes, dq, acc_q[at])
+                dk = jnp.where(keep_rows, dk, acc_kv[:, at])
+                dv = jnp.where(keep_rows, dv, acc_kv[:, at_v])
+            acc_o[at] = o
+            acc_q[at] = dq
+            acc_kv[:, at] = dk
+            acc_kv[:, at_v] = dv
 
     def dec_project(values, shown):
         x = jnp.where(shown > 0.5, values.astype(F32), blank)
@@ -374,20 +399,27 @@
     h_send[...] = placed
     halo_start(1, h_send, h_halo)
     x_mid, r_mid, qkv_mid = dec_project(placed, here)
-    window_block(split3(qkv_mid), dctx_mid, w_mid, None)
+    dec_b_copies = near_start(0, dec_b_send, dec_b, True)
+    window_block(split3(qkv_mid), dctx_mid, w_mid, None, None)
     halo_wait(1, h_send, h_halo)
-    _, _, qkv_low = dec_project(h_halo[0], vis_low)
-    window_block(split3(jnp.where(in_a, qkv_mid, qkv_low)), dctx_a, w_a, in_a)
-    _, _, qkv_high = dec_project(h_halo[1], vis_high)
-    window_block(split3(jnp.where(in_b, qkv_mid, qkv_high)), dctx_b, w_b, in_b)
-
-    near_columns(acc[:, 3 * width :].astype(BF), dec_a_send)
-    dec_a_copies = near_start(1, dec_a_send, dec_a, False)
-    dnormed = mm_nt(acc[:, : 3 * width].astype(BF), dec_qkv[...])
+    _, _, qkv_edge = dec_project(
+        h_halo[...].reshape(2 * tiles, width), jnp.concatenate([vis_low, vis_high], axis=0)
+    )
+    qkv_a = jnp.where(in_a, qkv_mid, qkv_edge[:tiles])
+    qkv_b = jnp.where(in_b, qkv_mid, qkv_edge[tiles:])
+    window_block(split3(qkv_a), dctx_a, w_a, in_a, at_a)
+    window_block(split3(qkv_b), dctx_b, w_b, in_b, at_b)
+
+    grad_q = (acc_q[...].T * scale).astype(BF)
+    dnormed = mm_nt(grad_q, dec_qkv[:, :width]) + mm_nt(
+        acc_kv[...].astype(BF), dec_qkv[:, width:]
+    )
     dinputs = norm_back(x_mid, r_mid, dnormed) + grad_out.astype(F32)
     sbuf[2] = pack(mm_tn(by_tile, dinputs.astype(BF)), groups)
     all_to_all_start(2)
 
+    near_columns(acc_o[...].astype(BF), dec_a_send, mm_tn)
+    dec_a_copies = near_start(1, dec_a_send, dec_a, False)
     for copy in dec_a_copies + dec_b_copies:
         copy.wait_recv()
     dec_own, dec_far = far_start(0, near_product(dec_a, dec_b))
@@ -398,11 +430,11 @@
         enc_b_send[j] = grad_enc_b[:, j * cw : (j + 1) * cw]
     enc_copies = near_start(2, enc_a_send, enc_a, False) + near_start(3, enc_b_send, enc_b, True)
     dox = spread(mm_nt(grad_enc_b, enc_out[...]).astype(BF))
-    dp = mm_nt(dox, v).astype(BF).astype(F32)
-    dsb = (enc_p * (dp - jnp.sum(enc_p * dp, axis=-1, keepdims=True)) * scale).astype(BF)
-    dq = gather_heads(mm(dsb, k))
-    dk = mm_tn(dsb, qx)
-    dv = mm_tn(enc_pb, dox)
+    dp = mm_nt(v, dox)
+    dsb = (enc_p * (dp - jnp.sum(enc_p * dp, axis=0, keepdims=True)) * scale).astype(BF)
+    dq = gather_heads(mm_tn(dsb, k))
+    dk = mm(dsb, qx)
+    dv = mm(enc_pb, dox)
     dproj = jnp.concatenate([dq, dk, dv], axis=1).astype(BF)
     dn = mm_nt(dproj, enc_qkv[...]).astype(BF).astype(F32)
     dtok = (norm_back(tok, tok_r, dn) + grad_enc).astype(BF)
@@ -417,7 +449,7 @@
     out_enc[...] = far_end(enc_own, enc_far, 1)
     for copy in pending:
         copy.wait_send()
-    halo_end(0, og.at[0], og_halo)
+    halo_end(0, og, og_halo)
     halo_end(1, h_send, h_halo)
 
 
@@ -439,9 +471,18 @@
             jax.ShapeDtypeStruct((rb, cw), F32),
             jax.ShapeDtypeStruct((rb, cw), F32),
         ),
-        in_specs=[vmem] * 9,
+        in_specs=[pl.BlockSpec(memory_space=pl.ANY)] * 9,
         out_specs=(vmem,) * 3,
         scratch_shapes=[
+            pltpu.VMEM((tiles, width), BF),
+            pltpu.VMEM(vis.shape, I32),
+            pltpu.VMEM(win.shape, I32),
+            pltpu.VMEM((tiles, width), BF),
+            pltpu.VMEM((1, width), F32),
+            pltpu.VMEM(enc_qkv.shape, BF),
+            pltpu.VMEM(enc_out.shape, BF),
+            pltpu.VMEM(dec_qkv.shape, BF),
+            pltpu.VMEM(dec_out.shape, BF),
             pltpu.VMEM((4, groups, 2 * CAP, width // 2), BF),
             pltpu.VMEM((4, groups, 2 * CAP, width // 2), BF),
             pltpu.VMEM((2, tiles, width), BF),
@@ -458,14 +499,17 @@
             pltpu.VMEM((2, far, rb, cw), far_type),
             pltpu.VMEM((2, far, rb, cw), far_type),
             pltpu.VMEM((far, rb, cw), F32),
-            pltpu.VMEM((tiles, 4 * width), F32),
+            pltpu.VMEM((width, tiles), F32),
+            pltpu.VMEM((tiles, 2 * width), F32),
+            pltpu.VMEM((width, tiles), F32),
+            dma((9,)),
             dma((4, groups)), dma((4, groups)),
             dma((2, 2)), dma((2, 2)),
             dma((4, ns)), dma((4, ns)),
             dma((2, far)), dma((2, far)),
         ],
         compiler_params=pltpu.CompilerParams(
-            collective_id=0, has_side_effects=True, vmem_limit_bytes=44 * 1024 * 1024
+            collective_id=0, has_side_effects=True, vmem_limit_bytes=60 * 1024 * 1024
         ),
     )(emb, vis, win, og, mask_token[None, :], enc_qkv, enc_out, dec_qkv, dec_out)
 

time: 57.2 us -> 51.9 us (0.907)
  local copies, waits for them, and re-layouts: 10.6 us -> 4.32 us
  Pallas kernels: 45.6 us -> 46.7 us
    unnamed x21 -> x3, local copies, waits for them, and re-layouts: 10.6 us -> 4.32 us
    pallas_call x1, Pallas kernels: 45.6 us -> 46.7 us  [shards(): pl.pallas_call(functools.partial(kernel, groups, slides, near), out_shape...]
where the time goes in v2:
time: 51.9 us; the launch traced here: 51.6 us
  Pallas kernels  46.7 us (90%)
  local copies, waits for them, and re-layouts  4.32 us (8%)
  between operations  0.64 us (1%)
    pallas_call x1, Pallas kernels, shards(): pl.pallas_call(functools.partial(kernel, groups, slides, near), out_shape...  46.7 us
    unnamed x3, local copies, waits for them, and re-layouts  4.32 us

profile of v2, /device:TPU:0, one launch (start us, length us, event | category | flops | bytes accessed | tf_op | source)
XLA Modules:
  0.0 51.6 jit_solution(4495703424925644568)
XLA Ops:
  0.6 46.7 %shard_map.112 = (bf16[1,128,512]{2,1,0:T(8,128)(2,1)}, f32[32,256]{1,0:T(8,128)}, f32[32,256]{1,0:T(8,128)}) custom-call(bf16[1,128,512]{2,1,0:T(8,128)(2,1)} %emb_in.1, s32[1,512]{1,0:T(1,128)} %vis_in.1, s32[1,2048]{1,0:T(1,128)} %win_in.1, bf16[1,128,512]{2,1,0:T(8,128)(2,1)} %og_in.1, f32[1,512]{1,0:T(1,128)} %bitcast.1, bf16[512,1536]{1,0:T(8,128)(2,1)} %enc_qkv_in.1, ...), custom_call_target="tpu_custom_call" | custom-call | tf_op jit(solution)/shard_map/pallas_call | solution.py:467
  47.3 1.6 %copy.15 = bf16[1,128,512]{2,1,0:T(8,128)(2,1)} copy(bf16[1,128,512]{2,1,0:T(8,128)(2,1)} %get-tuple-element.6) | data formatting | bytes 262144
  48.9 1.4 %copy.16 = f32[32,256]{1,0:T(8,128)} copy(f32[32,256]{1,0:T(8,128)} %get-tuple-element.7) | data formatting | bytes 65536
  50.2 1.4 %copy.17 = f32[32,256]{1,0:T(8,128)} copy(f32[32,256]{1,0:T(8,128)} %get-tuple-element.8) | data formatting | bytes 65536

commit v3 on v2

--- a/solution.py
+++ b/solution.py
@@ -42,22 +42,20 @@
     return r * dn - x * (r * r * r * jnp.mean(dn * x, axis=-1, keepdims=True))
 
 
-def pack(rows, peers):
-    width = rows.shape[1]
-    cube = rows.reshape(peers, CAP, width)
-    halves = [cube[:, :, : width // 2], cube[:, :, width // 2 :]]
-    return jnp.concatenate(halves, axis=1).astype(BF)
-
-
-def unpack(cube):
-    peers, rows, half = cube.shape
-    wide = cube.astype(F32)
-    wide = jnp.concatenate([wide[:, :CAP], wide[:, CAP:]], axis=2)
-    return wide.reshape(peers * CAP, 2 * half).astype(BF)
-
-
-def one_hot(ids, count):
-    return jnp.where(iota((ids.shape[0], count), 1) == ids, 1.0, 0.0).astype(BF)
+def fold(rows):
+    half = rows.shape[1] // 2
+    return jnp.concatenate([rows[:, :half], rows[:, half:]], axis=0)
+
+
+def unfold(rows):
+    n = rows.shape[0] // 2
+    return jnp.concatenate([rows[:n], rows[n:]], axis=1)
+
+
+def one_hot(peer, place, count):
+    left = peer * (2 * CAP) + place
+    ids = jnp.concatenate([left, left + jnp.where(peer < 0, 0, CAP)], axis=0)
+    return jnp.where(iota((ids.shape[0], 2 * CAP * count), 1) == ids, 1.0, 0.0).astype(BF)
 
 
 def as_columns(row):
@@ -142,7 +140,7 @@
                 send_sem=a2a_ss.at[stage, j], recv_sem=a2a_rs.at[stage, j],
                 device_id=(s, src), device_id_type=MESH,
             ).wait_recv()
-        return unpack(rbuf[stage])
+        return rbuf[stage].reshape(groups * 2 * CAP, width // 2)
 
     def halo_copies(kind, src, dst):
         left = jnp.maximum(g - 1, 0)
@@ -247,12 +245,19 @@
 
     rank = jnp.sum(jnp.where(vis_row < t_col, 1.0, 0.0), axis=1, keepdims=True).astype(I32)
     here = is_visible(t_col)
-    slot = jnp.bitwise_and(rank, groups - 1) * CAP + jnp.bitwise_and(
-        jnp.right_shift(rank, log_g), CAP - 1
-    )
-    by_tile = one_hot(jnp.where(here > 0.5, slot, -1), groups * CAP)
+    peer = jnp.where(here > 0.5, jnp.bitwise_and(rank, groups - 1), -1)
+    place = jnp.bitwise_and(jnp.right_shift(rank, log_g), CAP - 1)
+    by_tile = one_hot(peer, place, groups)
+
+    def to_slots(stage, by_row, rows):
+        moved = mm_tn(by_row, fold(rows)).astype(BF)
+        sbuf[stage] = moved.reshape(groups, 2 * CAP, width // 2)
+
+    def from_slots(by_row, slots):
+        return unfold(mm(by_row, slots))
+
     loaded(emb)
-    sbuf[0] = pack(mm_tn(by_tile, emb[...]), groups)
+    to_slots(0, by_tile, emb[...])
 
     pl.semaphore_wait(barrier, met)
     all_to_all_start(0)
@@ -265,9 +270,7 @@
         jnp.where(mine, vis_row.astype(F32), 0.0), axis=1, keepdims=True
     ).astype(I32)
     source = jnp.right_shift(token_tile, tiles.bit_length() - 1)
-    by_token = one_hot(
-        source * CAP + jnp.bitwise_and(iota((tokens, 1), 0), CAP - 1), groups * CAP
-    )
+    by_token = one_hot(source, jnp.bitwise_and(iota((tokens, 1), 0), CAP - 1), groups)
     grad_out = og[...]
     for k in range(slides):
         dec_b_send[k] = grad_out[:, k * cw : (k + 1) * cw]
@@ -290,7 +293,7 @@
     loaded(enc_qkv, enc_out, win, mask_token, dec_qkv)
     slots = all_to_all_wait(0)
 
-    tok = mm(by_token, slots)
+    tok = from_slots(by_token, slots)
     tok_r = norm_scale(tok)
     proj = mm((tok * tok_r).astype(BF), enc_qkv[...]).astype(BF)
     q, k, v = proj[:, :width], proj[:, width : 2 * width], proj[:, 2 * width :]
@@ -317,7 +320,7 @@
     enc_pb = enc_p.astype(BF)
     enc_ctx = gather_heads(mm_tn(enc_pb, v)).astype(BF)
     encoded = (tok + mm(enc_ctx, enc_out[...])).astype(BF)
-    sbuf[1] = pack(mm_tn(by_token, encoded), groups)
+    to_slots(1, by_token, encoded)
     all_to_all_start(1)
 
     w_mid = win[:, pl.ds(pl.multiple_of(g * tiles, tiles), tiles)]
@@ -395,7 +398,7 @@
         return values[:, :width], values[:, width : 2 * width], values[:, 2 * width :]
 
     slots = all_to_all_wait(1)
-    placed = mm(by_tile, slots).astype(BF)
+    placed = from_slots(by_tile, slots).astype(BF)
     h_send[...] = placed
     halo_start(1, h_send, h_halo)
     x_mid, r_mid, qkv_mid = dec_project(placed, here)
@@ -415,16 +418,12 @@
         acc_kv[...].astype(BF), dec_qkv[:, width:]
     )
     dinputs = norm_back(x_mid, r_mid, dnormed) + grad_out.astype(F32)
-    sbuf[2] = pack(mm_tn(by_tile, dinputs.astype(BF)), groups)
+    to_slots(2, by_tile, dinputs.astype(BF))
     all_to_all_start(2)
 
     near_columns(acc_o[...].astype(BF), dec_a_send, mm_tn)
     dec_a_copies = near_start(1, dec_a_send, dec_a, False)
-    for copy in dec_a_copies + dec_b_copies:
-        copy.wait_recv()
-    dec_own, dec_far = far_start(0, near_product(dec_a, dec_b))
-
-    grad_enc = mm(by_token, all_to_all_wait(2))
+    grad_enc = from_slots(by_token, all_to_all_wait(2))
     grad_enc_b = grad_enc.astype(BF)
     for j in range(slides):
         enc_b_send[j] = grad_enc_b[:, j * cw : (j + 1) * cw]
@@ -438,19 +437,31 @@
     dproj = jnp.concatenate([dq, dk, dv], axis=1).astype(BF)
     dn = mm_nt(dproj, enc_qkv[...]).astype(BF).astype(F32)
     dtok = (norm_back(tok, tok_r, dn) + grad_enc).astype(BF)
-    sbuf[3] = pack(mm_tn(by_token, dtok), groups)
+    to_slots(3, by_token, dtok)
     all_to_all_start(3)
 
-    out_dec[...] = far_end(dec_own, dec_far, 0)
+    for copy in dec_a_copies + dec_b_copies:
+        copy.wait_recv()
+    dec_own, dec_far = far_start(0, near_product(dec_a, dec_b))
     for copy in enc_copies:
         copy.wait_recv()
     enc_own, enc_far = far_start(1, near_product(enc_a, enc_b))
-    out_tiles[0] = mm(by_tile, all_to_all_wait(3)).astype(BF)
+    out_tiles[0] = from_slots(by_tile, all_to_all_wait(3)).astype(BF)
+    out_dec[...] = far_end(dec_own, dec_far, 0)
     out_enc[...] = far_end(enc_own, enc_far, 1)
     for copy in pending:
         copy.wait_send()
     halo_end(0, og, og_halo)
     halo_end(1, h_send, h_halo)
+
+
+def hand_over(a, b, c, a_out, b_out, c_out, sems):
+    pairs = ((a, a_out), (b, b_out), (c, c_out))
+    copies = [pltpu.make_async_copy(x, y, sems.at[i]) for i, (x, y) in enumerate(pairs)]
+    for copy in copies:
+        copy.start()
+    for copy in copies:
+        copy.wait()
 
 
 def shards(groups, slides, emb, vis, win, og, mask_token, enc_qkv, enc_out, dec_qkv, dec_out):
@@ -464,7 +475,7 @@
     far_type = BF if rb % 16 == 0 else F32
     dma = pltpu.SemaphoreType.DMA
     vmem = pl.BlockSpec(memory_space=pltpu.VMEM)
-    return pl.pallas_call(
+    results = pl.pallas_call(
         functools.partial(kernel, groups, slides, near),
         out_shape=(
             jax.ShapeDtypeStruct(emb.shape, BF),
@@ -512,6 +523,13 @@
             collective_id=0, has_side_effects=True, vmem_limit_bytes=60 * 1024 * 1024
         ),
     )(emb, vis, win, og, mask_token[None, :], enc_qkv, enc_out, dec_qkv, dec_out)
+    return pl.pallas_call(
+        hand_over,
+        out_shape=tuple(jax.ShapeDtypeStruct(r.shape, r.dtype) for r in results),
+        in_specs=[pl.BlockSpec(memory_space=pl.ANY)] * 3,
+        out_specs=(pl.BlockSpec(memory_space=pltpu.HBM),) * 3,
+        scratch_shapes=[dma((3,))],
+    )(*results)
 
 
 def solution(mesh):

time: 51.9 us -> 54.6 us (1.052)
  Pallas kernels: 46.7 us -> 53.8 us
  local copies, waits for them, and re-layouts: 4.32 us -> 0 us
    pallas_call x0 -> x1, Pallas kernels: none -> 7.09 us  [shards(): pl.pallas_call(hand_over, out_shape=tuple((jax.ShapeDtypeStruct(r.shape,...]
    unnamed x3 -> x0, local copies, waits for them, and re-layouts: 4.32 us -> none
where the time goes in v3:
time: 54.6 us; the launch traced here: 54.5 us
  Pallas kernels  53.8 us (99%)
  between operations  0.64 us (1%)
    pallas_call x1, Pallas kernels, shards(): pl.pallas_call(functools.partial(kernel, groups, slides, near), out_shape...  46.8 us
    pallas_call x1, Pallas kernels, shards(): pl.pallas_call(hand_over, out_shape=tuple((jax.ShapeDtypeStruct(r.shape,...  7.09 us

profile of v3, /device:TPU:0, one launch (start us, length us, event | category | flops | bytes accessed | tf_op | source)
XLA Modules:
  0.0 54.5 jit_solution(9256653646025468671)
XLA Ops:
  0.6 46.8 %shard_map.112 = (bf16[1,128,512]{2,1,0:T(8,128)(2,1)}, f32[32,256]{1,0:T(8,128)}, f32[32,256]{1,0:T(8,128)}) custom-call(bf16[1,128,512]{2,1,0:T(8,128)(2,1)} %emb_in.1, s32[1,512]{1,0:T(1,128)} %vis_in.1, s32[1,2048]{1,0:T(1,128)} %win_in.1, bf16[1,128,512]{2,1,0:T(8,128)(2,1)} %og_in.1, f32[1,512]{1,0:T(1,128)} %bitcast.1, bf16[512,1536]{1,0:T(8,128)(2,1)} %enc_qkv_in.1, ...), custom_call_target="tpu_custom_call" | custom-call | tf_op jit(solution)/shard_map/pallas_call | solution.py:478
  47.4 7.1 %shard_map.113 = (bf16[1,128,512]{2,1,0:T(8,128)(2,1)}, f32[32,256]{1,0:T(8,128)}, f32[32,256]{1,0:T(8,128)}) custom-call(bf16[1,128,512]{2,1,0:T(8,128)(2,1)} %get-tuple-element.6.a, f32[32,256]{1,0:T(8,128)} %get-tuple-element.7.b, f32[32,256]{1,0:T(8,128)} %get-tuple-element.8.c), custom_call_target="tpu_custom_call" | custom-call | tf_op jit(solution)/shard_map/pallas_call | solution.py:526

commit v4 on v3

--- a/solution.py
+++ b/solution.py
@@ -118,28 +118,20 @@
             device_id=peer, device_id_type=MESH,
         )
         copy.start()
-        return copy
+
+    def take(like, sem):
+        pltpu.make_async_copy(like, like, sem).wait()
 
     def all_to_all_start(stage):
-        copies = []
         for j in sorted(range(1, groups), key=lambda j: -min(j, groups - j)):
             dst = lax.rem(g + j, groups)
-            copies.append(
-                send(sbuf.at[stage, dst], rbuf.at[stage, g], a2a_ss.at[stage, j],
-                     a2a_rs.at[stage, j], (s, dst))
-            )
+            send(sbuf.at[stage, dst], rbuf.at[stage, g], a2a_ss.at[stage], a2a_rs.at[stage],
+                 (s, dst))
         rbuf[stage, g] = sbuf[stage, g]
-        pending.extend(copies)
-        return copies
+        pending.append((sbuf.at[stage, pl.ds(0, groups - 1)], a2a_ss.at[stage]))
 
     def all_to_all_wait(stage):
-        for j in range(1, groups):
-            src = lax.rem(g + groups - j, groups)
-            pltpu.make_async_remote_copy(
-                src_ref=sbuf.at[stage, src], dst_ref=rbuf.at[stage, src],
-                send_sem=a2a_ss.at[stage, j], recv_sem=a2a_rs.at[stage, j],
-                device_id=(s, src), device_id_type=MESH,
-            ).wait_recv()
+        take(rbuf.at[stage, pl.ds(0, groups - 1)], a2a_rs.at[stage])
         return rbuf[stage].reshape(groups * 2 * CAP, width // 2)
 
     def halo_copies(kind, src, dst):
@@ -196,7 +188,6 @@
             to_right.wait_send()
 
     def near_start(kind, src, dst, by_slide):
-        copies = []
         for ds in range(slides):
             for dn in range(near):
                 o = ds * near + dn
@@ -205,31 +196,30 @@
                 if o == 0:
                     dst[0] = part[...]
                 else:
-                    copies.append(
-                        send(part, dst.at[o], near_ss.at[kind, o], near_rs.at[kind, o],
-                             (s2, f * near + n2))
-                    )
-        pending.extend(copies)
-        return copies
+                    send(part, dst.at[o], near_ss.at[kind], near_rs.at[kind],
+                         (s2, f * near + n2))
+        pending.append((dst.at[pl.ds(1, slides * near - 1)], near_ss.at[kind]))
+
+    def near_wait(kind, dst):
+        take(dst.at[pl.ds(1, slides * near - 1)], near_rs.at[kind])
 
     def far_start(which, part):
         cube = part.reshape(far, rb, cw)
         far_own[...] = cube
         far_send[which] = cube.astype(far_send.dtype)
-        copies = []
         for df in range(1, far):
             f2 = lax.rem(f + df, far)
-            copies.append(
-                send(far_send.at[which, f2], far_recv.at[which, df], far_ss.at[which, df],
-                     far_rs.at[which, df], (s, f2 * near + n))
-            )
-        pending.extend(copies)
-        return far_own[f], copies
-
-    def far_end(own, copies, which):
+            send(far_send.at[which, f2], far_recv.at[which, df], far_ss.at[which],
+                 far_rs.at[which], (s, f2 * near + n))
+        if far > 1:
+            pending.append((far_send.at[which, pl.ds(1, far - 1)], far_ss.at[which]))
+        return far_own[f]
+
+    def far_end(own, which):
+        if far > 1:
+            take(far_recv.at[which, pl.ds(1, far - 1)], far_rs.at[which])
         total = own
-        for df, copy in enumerate(copies, 1):
-            copy.wait_recv()
+        for df in range(1, far):
             total = total + far_recv[which, df].astype(F32)
         return total
 
@@ -402,7 +392,7 @@
     h_send[...] = placed
     halo_start(1, h_send, h_halo)
     x_mid, r_mid, qkv_mid = dec_project(placed, here)
-    dec_b_copies = near_start(0, dec_b_send, dec_b, True)
+    near_start(0, dec_b_send, dec_b, True)
     window_block(split3(qkv_mid), dctx_mid, w_mid, None, None)
     halo_wait(1, h_send, h_halo)
     _, _, qkv_edge = dec_project(
@@ -422,12 +412,13 @@
     all_to_all_start(2)
 
     near_columns(acc_o[...].astype(BF), dec_a_send, mm_tn)
-    dec_a_copies = near_start(1, dec_a_send, dec_a, False)
+    near_start(1, dec_a_send, dec_a, False)
     grad_enc = from_slots(by_token, all_to_all_wait(2))
     grad_enc_b = grad_enc.astype(BF)
     for j in range(slides):
         enc_b_send[j] = grad_enc_b[:, j * cw : (j + 1) * cw]
-    enc_copies = near_start(2, enc_a_send, enc_a, False) + near_start(3, enc_b_send, enc_b, True)
+    near_start(2, enc_a_send, enc_a, False)
+    near_start(3, enc_b_send, enc_b, True)
     dox = spread(mm_nt(grad_enc_b, enc_out[...]).astype(BF))
     dp = mm_nt(v, dox)
     dsb = (enc_p * (dp - jnp.sum(enc_p * dp, axis=0, keepdims=True)) * scale).astype(BF)
@@ -440,28 +431,19 @@
     to_slots(3, by_token, dtok)
     all_to_all_start(3)
 
-    for copy in dec_a_copies + dec_b_copies:
-        copy.wait_recv()
-    dec_own, dec_far = far_start(0, near_product(dec_a, dec_b))
-    for copy in enc_copies:
-        copy.wait_recv()
-    enc_own, enc_far = far_start(1, near_product(enc_a, enc_b))
+    near_wait(0, dec_b)
+    near_wait(1, dec_a)
+    dec_own = far_start(0, near_product(dec_a, dec_b))
+    near_wait(2, enc_a)
+    near_wait(3, enc_b)
+    enc_own = far_start(1, near_product(enc_a, enc_b))
     out_tiles[0] = from_slots(by_tile, all_to_all_wait(3)).astype(BF)
-    out_dec[...] = far_end(dec_own, dec_far, 0)
-    out_enc[...] = far_end(enc_own, enc_far, 1)
-    for copy in pending:
-        copy.wait_send()
+    out_dec[...] = far_end(dec_own, 0)
+    out_enc[...] = far_end(enc_own, 1)
+    for like, sem in pending:
+        take(like, sem)
     halo_end(0, og, og_halo)
     halo_end(1, h_send, h_halo)
-
-
-def hand_over(a, b, c, a_out, b_out, c_out, sems):
-    pairs = ((a, a_out), (b, b_out), (c, c_out))
-    copies = [pltpu.make_async_copy(x, y, sems.at[i]) for i, (x, y) in enumerate(pairs)]
-    for copy in copies:
-        copy.start()
-    for copy in copies:
-        copy.wait()
 
 
 def shards(groups, slides, emb, vis, win, og, mask_token, enc_qkv, enc_out, dec_qkv, dec_out):
@@ -474,8 +456,12 @@
     ns = near * slides
     far_type = BF if rb % 16 == 0 else F32
     dma = pltpu.SemaphoreType.DMA
+    operands = [
+        pltpu.with_memory_space_constraint(x, pltpu.HBM)
+        for x in (emb, vis, win, og, mask_token[None, :], enc_qkv, enc_out, dec_qkv, dec_out)
+    ]
     vmem = pl.BlockSpec(memory_space=pltpu.VMEM)
-    results = pl.pallas_call(
+    return pl.pallas_call(
         functools.partial(kernel, groups, slides, near),
         out_shape=(
             jax.ShapeDtypeStruct(emb.shape, BF),
@@ -514,22 +500,15 @@
             pltpu.VMEM((tiles, 2 * width), F32),
             pltpu.VMEM((width, tiles), F32),
             dma((9,)),
-            dma((4, groups)), dma((4, groups)),
+            dma((4,)), dma((4,)),
             dma((2, 2)), dma((2, 2)),
-            dma((4, ns)), dma((4, ns)),
-            dma((2, far)), dma((2, far)),
+            dma((4,)), dma((4,)),
+            dma((2,)), dma((2,)),
         ],
         compiler_params=pltpu.CompilerParams(
-            collective_id=0, has_side_effects=True, vmem_limit_bytes=60 * 1024 * 1024
+            collective_id=0, has_side_effects=True, vmem_limit_bytes=44 * 1024 * 1024
         ),
-    )(emb, vis, win, og, mask_token[None, :], enc_qkv, enc_out, dec_qkv, dec_out)
-    return pl.pallas_call(
-        hand_over,
-        out_shape=tuple(jax.ShapeDtypeStruct(r.shape, r.dtype) for r in results),
-        in_specs=[pl.BlockSpec(memory_space=pl.ANY)] * 3,
-        out_specs=(pl.BlockSpec(memory_space=pltpu.HBM),) * 3,
-        scratch_shapes=[dma((3,))],
-    )(*results)
+    )(*operands)
 
 
 def solution(mesh):

time: 54.6 us -> 46.9 us (0.86)
  Pallas kernels: 53.8 us -> 44.2 us
  local copies, waits for them, and re-layouts: 0 us -> 1.89 us
    pallas_call x1 -> x0, Pallas kernels: 7.09 us -> none  [shards(): pl.pallas_call(hand_over, out_shape=tuple((jax.ShapeDtypeStruct(r.shape,...]
    pallas_call x1, Pallas kernels: 46.8 us -> 44.2 us  [shards(): pl.pallas_call(functools.partial(kernel, groups, slides, near), out_shape...]
    unnamed x0 -> x3, local copies, waits for them, and re-layouts: none -> 1.89 us
where the time goes in v4:
time: 46.9 us; the launch traced here: 46.8 us
  Pallas kernels  44.2 us (94%)
  local copies, waits for them, and re-layouts  1.89 us (4%)
  between operations  0.64 us (1%)
    pallas_call x1, Pallas kernels, shards(): pl.pallas_call(functools.partial(kernel, groups, slides, near), out_shape...  44.2 us
    unnamed x3, local copies, waits for them, and re-layouts  1.89 us

profile of v4, /device:TPU:0, one launch (start us, length us, event | category | flops | bytes accessed | tf_op | source)
XLA Modules:
  0.0 46.8 jit_solution(2064054066706083687)
XLA Ops:
  0.6 44.2 %shard_map.112 = (bf16[1,128,512]{2,1,0:T(8,128)(2,1)S(1)}, f32[32,256]{1,0:T(8,128)S(1)}, f32[32,256]{1,0:T(8,128)S(1)}) custom-call(bf16[1,128,512]{2,1,0:T(8,128)(2,1)} %emb_in.1, s32[1,512]{1,0:T(1,128)} %vis_in.1, s32[1,2048]{1,0:T(1,128)} %win_in.1, bf16[1,128,512]{2,1,0:T(8,128)(2,1)} %og_in.1, f32[1,512]{1,0:T(1,128)} %bitcast.1, ...), custom_call_target="tpu_custom_call" | custom-call | tf_op jit(solution)/shard_map/pallas_call | solution.py:464
  44.9 0.7 %copy.15 = bf16[1,128,512]{2,1,0:T(8,128)(2,1)} copy(bf16[1,128,512]{2,1,0:T(8,128)(2,1)S(1)} %get-tuple-element.6) | data formatting | bytes 262144
  45.5 0.6 %copy.16 = f32[32,256]{1,0:T(8,128)} copy(f32[32,256]{1,0:T(8,128)S(1)} %get-tuple-element.7) | data formatting | bytes 65536
  46.2 0.6 %copy.17 = f32[32,256]{1,0:T(8,128)} copy(f32[32,256]{1,0:T(8,128)S(1)} %get-tuple-element.8) | data formatting | bytes 65536

commit v5 on v4

--- a/solution.py
+++ b/solution.py
@@ -92,7 +92,11 @@
         (dec_qkv_in, dec_qkv),
     )):
         loads.append((dst, pltpu.make_async_copy(src, dst, load_s.at[i])))
-        loads[i][1].start()
+    for _, copy in loads[:3]:
+        copy.start()
+
+    def wrap(index, count):
+        return index - count * jnp.minimum(jnp.maximum(index - (count - 1), 0), 1)
 
     def loaded(*refs):
         for dst, copy in loads:
@@ -103,12 +107,12 @@
     met = 0
     for j in range(1, groups):
         pl.semaphore_signal(
-            barrier, inc=1, device_id=(s, lax.rem(g + j, groups)), device_id_type=MESH
+            barrier, inc=1, device_id=(s, wrap(g + j, groups)), device_id_type=MESH
         )
         met += 1
     for ds in range(1, slides):
         for dn in range(near):
-            peer = (lax.rem(s + ds, slides), f * near + lax.rem(n + dn, near))
+            peer = (wrap(s + ds, slides), f * near + wrap(n + dn, near))
             pl.semaphore_signal(barrier, inc=1, device_id=peer, device_id_type=MESH)
             met += 1
 
@@ -124,7 +128,7 @@
 
     def all_to_all_start(stage):
         for j in sorted(range(1, groups), key=lambda j: -min(j, groups - j)):
-            dst = lax.rem(g + j, groups)
+            dst = wrap(g + j, groups)
             send(sbuf.at[stage, dst], rbuf.at[stage, g], a2a_ss.at[stage], a2a_rs.at[stage],
                  (s, dst))
         rbuf[stage, g] = sbuf[stage, g]
@@ -191,7 +195,7 @@
         for ds in range(slides):
             for dn in range(near):
                 o = ds * near + dn
-                s2, n2 = lax.rem(s + ds, slides), lax.rem(n + dn, near)
+                s2, n2 = wrap(s + ds, slides), wrap(n + dn, near)
                 part = src.at[s2] if by_slide else src.at[n2]
                 if o == 0:
                     dst[0] = part[...]
@@ -208,7 +212,7 @@
         far_own[...] = cube
         far_send[which] = cube.astype(far_send.dtype)
         for df in range(1, far):
-            f2 = lax.rem(f + df, far)
+            f2 = wrap(f + df, far)
             send(far_send.at[which, f2], far_recv.at[which, df], far_ss.at[which],
                  far_rs.at[which], (s, f2 * near + n))
         if far > 1:
@@ -247,6 +251,8 @@
         return unfold(mm(by_row, slots))
 
     loaded(emb)
+    for _, copy in loads[3:]:
+        copy.start()
     to_slots(0, by_tile, emb[...])
 
     pl.semaphore_wait(barrier, met)
@@ -280,13 +286,6 @@
         for k in range(near):
             dst[k] = moved[:, k * span : (k + 1) * span]
 
-    loaded(enc_qkv, enc_out, win, mask_token, dec_qkv)
-    slots = all_to_all_wait(0)
-
-    tok = from_slots(by_token, slots)
-    tok_r = norm_scale(tok)
-    proj = mm((tok * tok_r).astype(BF), enc_qkv[...]).astype(BF)
-    q, k, v = proj[:, :width], proj[:, width : 2 * width], proj[:, 2 * width :]
     head_width = width // HEADS
     scale = 1.0 / math.sqrt(head_width)
     rows = HEADS * tokens
@@ -297,6 +296,13 @@
     )
     heads_b = heads.astype(BF)
 
+    loaded(enc_qkv, enc_out, win, mask_token, dec_qkv)
+    slots = all_to_all_wait(0)
+
+    tok = from_slots(by_token, slots)
+    tok_r = norm_scale(tok)
+    proj = mm((tok * tok_r).astype(BF), enc_qkv[...]).astype(BF)
+    q, k, v = proj[:, :width], proj[:, width : 2 * width], proj[:, 2 * width :]
     def spread(values):
         return jnp.concatenate([values] * HEADS, axis=0) * heads_b
 
@@ -329,8 +335,8 @@
     blank = mask_token[...]
     near_columns(enc_ctx, enc_a_send)
     halo_wait(0, og, og_halo)
-    dctx_low = mm_nt(og_halo[0], dec_out[...])
-    dctx_high = mm_nt(og_halo[1], dec_out[...])
+    dctx_edge = mm_nt(og_halo[...].reshape(2 * tiles, width), dec_out[...])
+    dctx_low, dctx_high = dctx_edge[:tiles], dctx_edge[tiles:]
     dctx_a = jnp.where(in_a, dctx_mid.astype(F32), dctx_low).astype(BF)
     dctx_b = jnp.where(in_b, dctx_mid.astype(F32), dctx_high).astype(BF)
     lane = iota((1, 2 * head_width), 1)
@@ -392,9 +398,9 @@
     h_send[...] = placed
     halo_start(1, h_send, h_halo)
     x_mid, r_mid, qkv_mid = dec_project(placed, here)
-    near_start(0, dec_b_send, dec_b, True)
     window_block(split3(qkv_mid), dctx_mid, w_mid, None, None)
     halo_wait(1, h_send, h_halo)
+    near_start(0, dec_b_send, dec_b, True)
     _, _, qkv_edge = dec_project(
         h_halo[...].reshape(2 * tiles, width), jnp.concatenate([vis_low, vis_high], axis=0)
     )

time: 46.9 us -> 44.8 us (0.955)
  Pallas kernels: 44.2 us -> 42.1 us
    pallas_call x1, Pallas kernels: 44.2 us -> 42.1 us  [shards(): pl.pallas_call(functools.partial(kernel, groups, slides, near), out_shape...]
where the time goes in v5:
time: 44.8 us; the launch traced here: 44.6 us
  Pallas kernels  42.1 us (94%)
  local copies, waits for them, and re-layouts  1.89 us (4%)
  between operations  0.64 us (1%)
    pallas_call x1, Pallas kernels, shards(): pl.pallas_call(functools.partial(kernel, groups, slides, near), out_shape...  42.1 us
    unnamed x3, local copies, waits for them, and re-layouts  1.89 us

profile of v5, /device:TPU:0, one launch (start us, length us, event | category | flops | bytes accessed | tf_op | source)
XLA Modules:
  0.0 44.6 jit_solution(15299304131432187826)
XLA Ops:
  0.6 42.1 %shard_map.112 = (bf16[1,128,512]{2,1,0:T(8,128)(2,1)S(1)}, f32[32,256]{1,0:T(8,128)S(1)}, f32[32,256]{1,0:T(8,128)S(1)}) custom-call(bf16[1,128,512]{2,1,0:T(8,128)(2,1)} %emb_in.1, s32[1,512]{1,0:T(1,128)} %vis_in.1, s32[1,2048]{1,0:T(1,128)} %win_in.1, bf16[1,128,512]{2,1,0:T(8,128)(2,1)} %og_in.1, f32[1,512]{1,0:T(1,128)} %bitcast.1, ...), custom_call_target="tpu_custom_call" | custom-call | tf_op jit(solution)/shard_map/pallas_call | solution.py:470
  42.8 0.7 %copy.15 = bf16[1,128,512]{2,1,0:T(8,128)(2,1)} copy(bf16[1,128,512]{2,1,0:T(8,128)(2,1)S(1)} %get-tuple-element.6) | data formatting | bytes 262144
  43.4 0.6 %copy.16 = f32[32,256]{1,0:T(8,128)} copy(f32[32,256]{1,0:T(8,128)S(1)} %get-tuple-element.7) | data formatting | bytes 65536
  44.0 0.6 %copy.17 = f32[32,256]{1,0:T(8,128)} copy(f32[32,256]{1,0:T(8,128)S(1)} %get-tuple-element.8) | data formatting | bytes 65536

commit v6 on v5

--- a/solution.py
+++ b/solution.py
@@ -71,7 +71,7 @@
     sbuf, rbuf, og_halo, h_send, h_halo,
     dec_a_send, dec_b_send, dec_a, dec_b,
     enc_a_send, enc_b_send, enc_a, enc_b,
-    far_send, far_recv, far_own, acc_q, acc_kv, acc_o, load_s,
+    far_send, far_recv, far_own, acc_q, acc_kv, probs, load_s,
     a2a_ss, a2a_rs, halo_ss, halo_rs, near_ss, near_rs, far_ss, far_rs,
 ):
     s = lax.axis_index("slide")
@@ -354,7 +354,7 @@
             [values[:head_width, :tiles], values[head_width:, tiles:]], axis=0
         )
 
-    def window_block(qkv, dctx, row, keep_rows, keep_lanes):
+    def window_block(block, qkv, dctx, row, keep_rows, keep_lanes):
         bias = same_window(row)
         for pair in range(HEADS // 2):
             at = slice(pair * 2 * head_width, (pair + 1) * 2 * head_width)
@@ -366,22 +366,31 @@
             e = jnp.exp(scores - jnp.max(scores, axis=0, keepdims=True))
             p = e * (1.0 / jnp.sum(e, axis=0, keepdims=True))
             pb = p.astype(BF)
+            probs[block, pair] = pb
             dp = mm_nt(vs, dox)
             dsb = (p * (dp - jnp.sum(p * dp, axis=0, keepdims=True))).astype(BF)
-            o = diagonal(mm_tn(vs, pb))
             dq = diagonal(mm_tn(ks, dsb))
             dk = mm(dsb, qx)
             dv = mm(pb, dox)
             at_v = slice(width + at.start, width + at.stop)
             if keep_rows is not None:
-                o = jnp.where(keep_lanes, o, acc_o[at])
                 dq = jnp.where(keep_lanes, dq, acc_q[at])
                 dk = jnp.where(keep_rows, dk, acc_kv[:, at])
                 dv = jnp.where(keep_rows, dv, acc_kv[:, at_v])
-            acc_o[at] = o
             acc_q[at] = dq
             acc_kv[:, at] = dk
             acc_kv[:, at_v] = dv
+
+    def window_context(values_of):
+        pairs = []
+        for pair in range(HEADS // 2):
+            at = slice(pair * 2 * head_width, (pair + 1) * 2 * head_width)
+            mid, low, high = [
+                diagonal(mm_tn(values[:, at], probs[block, pair]))
+                for block, values in enumerate(values_of)
+            ]
+            pairs.append(jnp.where(at_b, high, jnp.where(at_a, low, mid)))
+        return jnp.concatenate(pairs, axis=0).astype(BF)
 
     def dec_project(values, shown):
         x = jnp.where(shown > 0.5, values.astype(F32), blank)
@@ -398,7 +407,8 @@
     h_send[...] = placed
     halo_start(1, h_send, h_halo)
     x_mid, r_mid, qkv_mid = dec_project(placed, here)
-    window_block(split3(qkv_mid), dctx_mid, w_mid, None, None)
+    parts_mid = split3(qkv_mid)
+    window_block(0, parts_mid, dctx_mid, w_mid, None, None)
     halo_wait(1, h_send, h_halo)
     near_start(0, dec_b_send, dec_b, True)
     _, _, qkv_edge = dec_project(
@@ -406,8 +416,9 @@
     )
     qkv_a = jnp.where(in_a, qkv_mid, qkv_edge[:tiles])
     qkv_b = jnp.where(in_b, qkv_mid, qkv_edge[tiles:])
-    window_block(split3(qkv_a), dctx_a, w_a, in_a, at_a)
-    window_block(split3(qkv_b), dctx_b, w_b, in_b, at_b)
+    parts_a, parts_b = split3(qkv_a), split3(qkv_b)
+    window_block(1, parts_a, dctx_a, w_a, in_a, at_a)
+    window_block(2, parts_b, dctx_b, w_b, in_b, at_b)
 
     grad_q = (acc_q[...].T * scale).astype(BF)
     dnormed = mm_nt(grad_q, dec_qkv[:, :width]) + mm_nt(
@@ -417,7 +428,8 @@
     to_slots(2, by_tile, dinputs.astype(BF))
     all_to_all_start(2)
 
-    near_columns(acc_o[...].astype(BF), dec_a_send, mm_tn)
+    dec_ctx = window_context((parts_mid[2], parts_a[2], parts_b[2]))
+    near_columns(dec_ctx, dec_a_send, mm_tn)
     near_start(1, dec_a_send, dec_a, False)
     grad_enc = from_slots(by_token, all_to_all_wait(2))
     grad_enc_b = grad_enc.astype(BF)
@@ -452,6 +464,15 @@
     halo_end(1, h_send, h_halo)
 
 
+def hand_over(a, b, c, a_out, b_out, c_out, sems):
+    pairs = ((a, a_out), (b, b_out), (c, c_out))
+    copies = [pltpu.make_async_copy(x, y, sems.at[i]) for i, (x, y) in enumerate(pairs)]
+    for copy in copies:
+        copy.start()
+    for copy in copies:
+        copy.wait()
+
+
 def shards(groups, slides, emb, vis, win, og, mask_token, enc_qkv, enc_out, dec_qkv, dec_out):
     _, tiles, width = emb.shape
     tokens = vis.shape[1] // groups
@@ -467,7 +488,7 @@
         for x in (emb, vis, win, og, mask_token[None, :], enc_qkv, enc_out, dec_qkv, dec_out)
     ]
     vmem = pl.BlockSpec(memory_space=pltpu.VMEM)
-    return pl.pallas_call(
+    results = pl.pallas_call(
         functools.partial(kernel, groups, slides, near),
         out_shape=(
             jax.ShapeDtypeStruct(emb.shape, BF),
@@ -504,7 +525,7 @@
             pltpu.VMEM((far, rb, cw), F32),
             pltpu.VMEM((width, tiles), F32),
             pltpu.VMEM((tiles, 2 * width), F32),
-            pltpu.VMEM((width, tiles), F32),
+            pltpu.VMEM((3, HEADS // 2, tiles, 2 * tiles), BF),
             dma((9,)),
             dma((4,)), dma((4,)),
             dma((2, 2)), dma((2, 2)),
@@ -515,6 +536,13 @@
             collective_id=0, has_side_effects=True, vmem_limit_bytes=44 * 1024 * 1024
         ),
     )(*operands)
+    return pl.pallas_call(
+        hand_over,
+        out_shape=tuple(jax.ShapeDtypeStruct(r.shape, r.dtype) for r in results),
+        in_specs=[pl.BlockSpec(memory_space=pltpu.VMEM)] * 3,
+        out_specs=(pl.BlockSpec(memory_space=pltpu.HBM),) * 3,
+        scratch_shapes=[dma((3,))],
+    )(*results)
 
 
 def solution(mesh):

time: 44.8 us -> 46.8 us (1.045)
  Pallas kernels: 42.1 us -> 44.2 us
    pallas_call x0 -> x1, Pallas kernels: none -> 1.62 us  [shards(): pl.pallas_call(hand_over, out_shape=tuple((jax.ShapeDtypeStruct(r.shape,...]
    unnamed x3 -> x6, local copies, waits for them, and re-layouts: 1.89 us -> 1.84 us
where the time goes in v6:
time: 46.8 us; the launch traced here: 46.7 us
  Pallas kernels  44.2 us (94%)
  local copies, waits for them, and re-layouts  1.84 us (4%)
  between operations  0.65 us (1%)
    pallas_call x1, Pallas kernels, shards(): pl.pallas_call(functools.partial(kernel, groups, slides, near), out_shape...  42.6 us
    unnamed x6, local copies, waits for them, and re-layouts  1.84 us
    pallas_call x1, Pallas kernels, shards(): pl.pallas_call(hand_over, out_shape=tuple((jax.ShapeDtypeStruct(r.shape,...  1.62 us

profile of v6, /device:TPU:0, one launch (start us, length us, event | category | flops | bytes accessed | tf_op | source)
XLA Modules:
  0.0 46.7 jit_solution(4377602292075720437)
XLA Ops:
  0.6 42.6 %shard_map.112 = (bf16[1,128,512]{2,1,0:T(8,128)(2,1)S(1)}, f32[32,256]{1,0:T(8,128)S(1)}, f32[32,256]{1,0:T(8,128)S(1)}) custom-call(bf16[1,128,512]{2,1,0:T(8,128)(2,1)} %emb_in.1, s32[1,512]{1,0:T(1,128)} %vis_in.1, s32[1,2048]{1,0:T(1,128)} %win_in.1, bf16[1,128,512]{2,1,0:T(8,128)(2,1)} %og_in.1, f32[1,512]{1,0:T(1,128)} %bitcast.1, ...), custom_call_target="tpu_custom_call" | custom-call | tf_op jit(solution)/shard_map/pallas_call | solution.py:491
  43.2 0.0 copy-start
  43.2 0.6 %copy-done = bf16[1,128,512]{2,1,0:T(8,128)(2,1)} copy-done((bf16[1,128,512]{2,1,0:T(8,128)(2,1)}, bf16[1,128,512]{2,1,0:T(8,128)(2,1)S(1)}, u32[]{:S(2)}) %copy-start) | copy-done | bytes 131096
  43.8 0.0 copy-start.1
  43.9 0.6 %copy-done.1 = f32[32,256]{1,0:T(8,128)} copy-done((f32[32,256]{1,0:T(8,128)}, f32[32,256]{1,0:T(8,128)S(1)}, u32[]{:S(2)}) %copy-start.1) | copy-done | bytes 32792
  44.4 0.0 copy-start.2
  44.5 0.6 %copy-done.2 = f32[32,256]{1,0:T(8,128)} copy-done((f32[32,256]{1,0:T(8,128)}, f32[32,256]{1,0:T(8,128)S(1)}, u32[]{:S(2)}) %copy-start.2) | copy-done | bytes 32792
  45.1 1.6 %shard_map.113 = (bf16[1,128,512]{2,1,0:T(8,128)(2,1)}, f32[32,256]{1,0:T(8,128)}, f32[32,256]{1,0:T(8,128)}) custom-call(bf16[1,128,512]{2,1,0:T(8,128)(2,1)} %copy-done, f32[32,256]{1,0:T(8,128)} %copy-done.1, f32[32,256]{1,0:T(8,128)} %copy-done.2), custom_call_target="tpu_custom_call" | custom-call | tf_op jit(solution)/shard_map/pallas_call | solution.py:539
Async XLA Ops:
  43.2 0.6 %copy-start = (bf16[1,128,512]{2,1,0:T(8,128)(2,1)}, bf16[1,128,512]{2,1,0:T(8,128)(2,1)S(1)}, u32[]{:S(2)}) copy-start(bf16[1,128,512]{2,1,0:T(8,128)(2,1)S(1)} %get-tuple-element.6.a) | copy-start | bytes 393220
  43.8 0.6 %copy-start.1 = (f32[32,256]{1,0:T(8,128)}, f32[32,256]{1,0:T(8,128)S(1)}, u32[]{:S(2)}) copy-start(f32[32,256]{1,0:T(8,128)S(1)} %get-tuple-element.7.b) | copy-start | bytes 98308
  44.4 0.6 %copy-start.2 = (f32[32,256]{1,0:T(8,128)}, f32[32,256]{1,0:T(8,128)S(1)}, u32[]{:S(2)}) copy-start(f32[32,256]{1,0:T(8,128)S(1)} %get-tuple-element.8.c) | copy-start | bytes 98308

commit v7 on v6

--- a/solution.py
+++ b/solution.py
@@ -334,6 +334,7 @@
     vis_high = is_visible(t_col + tiles)
     blank = mask_token[...]
     near_columns(enc_ctx, enc_a_send)
+    near_start(2, enc_a_send, enc_a, False)
     halo_wait(0, og, og_halo)
     dctx_edge = mm_nt(og_halo[...].reshape(2 * tiles, width), dec_out[...])
     dctx_low, dctx_high = dctx_edge[:tiles], dctx_edge[tiles:]
@@ -354,9 +355,12 @@
             [values[:head_width, :tiles], values[head_width:, tiles:]], axis=0
         )
 
-    def window_block(block, qkv, dctx, row, keep_rows, keep_lanes):
-        bias = same_window(row)
-        for pair in range(HEADS // 2):
+    def window_blocks(*blocks):
+        biases = [same_window(row) for _, _, _, row, _, _ in blocks]
+        steps = [(pair, i) for pair in range(HEADS // 2) for i in range(len(blocks))]
+        for pair, i in steps:
+            block, qkv, dctx, _, keep_rows, keep_lanes = blocks[i]
+            bias = biases[i]
             at = slice(pair * 2 * head_width, (pair + 1) * 2 * head_width)
             qs, ks, vs = qkv[0][:, at], qkv[1][:, at], qkv[2][:, at]
             do = dctx[:, at]
@@ -408,7 +412,7 @@
     halo_start(1, h_send, h_halo)
     x_mid, r_mid, qkv_mid = dec_project(placed, here)
     parts_mid = split3(qkv_mid)
-    window_block(0, parts_mid, dctx_mid, w_mid, None, None)
+    window_blocks((0, parts_mid, dctx_mid, w_mid, None, None))
     halo_wait(1, h_send, h_halo)
     near_start(0, dec_b_send, dec_b, True)
     _, _, qkv_edge = dec_project(
@@ -417,8 +421,9 @@
     qkv_a = jnp.where(in_a, qkv_mid, qkv_edge[:tiles])
     qkv_b = jnp.where(in_b, qkv_mid, qkv_edge[tiles:])
     parts_a, parts_b = split3(qkv_a), split3(qkv_b)
-    window_block(1, parts_a, dctx_a, w_a, in_a, at_a)
-    window_block(2, parts_b, dctx_b, w_b, in_b, at_b)
+    window_blocks(
+        (1, parts_a, dctx_a, w_a, in_a, at_a), (2, parts_b, dctx_b, w_b, in_b, at_b)
+    )
 
     grad_q = (acc_q[...].T * scale).astype(BF)
     dnormed = mm_nt(grad_q, dec_qkv[:, :width]) + mm_nt(
@@ -435,7 +440,6 @@
     grad_enc_b = grad_enc.astype(BF)
     for j in range(slides):
         enc_b_send[j] = grad_enc_b[:, j * cw : (j + 1) * cw]
-    near_start(2, enc_a_send, enc_a, False)
     near_start(3, enc_b_send, enc_b, True)
     dox = spread(mm_nt(grad_enc_b, enc_out[...]).astype(BF))
     dp = mm_nt(v, dox)
@@ -462,15 +466,6 @@
         take(like, sem)
     halo_end(0, og, og_halo)
     halo_end(1, h_send, h_halo)
-
-
-def hand_over(a, b, c, a_out, b_out, c_out, sems):
-    pairs = ((a, a_out), (b, b_out), (c, c_out))
-    copies = [pltpu.make_async_copy(x, y, sems.at[i]) for i, (x, y) in enumerate(pairs)]
-    for copy in copies:
-        copy.start()
-    for copy in copies:
-        copy.wait()
 
 
 def shards(groups, slides, emb, vis, win, og, mask_token, enc_qkv, enc_out, dec_qkv, dec_out):
@@ -488,7 +483,7 @@
         for x in (emb, vis, win, og, mask_token[None, :], enc_qkv, enc_out, dec_qkv, dec_out)
     ]
     vmem = pl.BlockSpec(memory_space=pltpu.VMEM)
-    results = pl.pallas_call(
+    return pl.pallas_call(
         functools.partial(kernel, groups, slides, near),
         out_shape=(
             jax.ShapeDtypeStruct(emb.shape, BF),
@@ -536,13 +531,6 @@
             collective_id=0, has_side_effects=True, vmem_limit_bytes=44 * 1024 * 1024
         ),
     )(*operands)
-    return pl.pallas_call(
-        hand_over,
-        out_shape=tuple(jax.ShapeDtypeStruct(r.shape, r.dtype) for r in results),
-        in_specs=[pl.BlockSpec(memory_space=pltpu.VMEM)] * 3,
-        out_specs=(pl.BlockSpec(memory_space=pltpu.HBM),) * 3,
-        scratch_shapes=[dma((3,))],
-    )(*results)
 
 
 def solution(mesh):

time: 46.8 us -> 44.5 us (0.951)
  Pallas kernels: 44.2 us -> 41.8 us
    pallas_call x1 -> x0, Pallas kernels: 1.62 us -> none  [shards(): pl.pallas_call(hand_over, out_shape=tuple((jax.ShapeDtypeStruct(r.shape,...]
    pallas_call x1, Pallas kernels: 42.6 us -> 41.8 us  [shards(): pl.pallas_call(functools.partial(kernel, groups, slides, near), out_shape...]
    unnamed x6 -> x3, local copies, waits for them, and re-layouts: 1.84 us -> 1.89 us
where the time goes in v7:
time: 44.5 us; the launch traced here: 44.3 us
  Pallas kernels  41.8 us (94%)
  local copies, waits for them, and re-layouts  1.89 us (4%)
  between operations  0.64 us (1%)
    pallas_call x1, Pallas kernels, shards(): pl.pallas_call(functools.partial(kernel, groups, slides, near), out_shape...  41.8 us
    unnamed x3, local copies, waits for them, and re-layouts  1.89 us

profile of v7, /device:TPU:0, one launch (start us, length us, event | category | flops | bytes accessed | tf_op | source)
XLA Modules:
  0.0 44.3 jit_solution(3278261356793702762)
XLA Ops:
  0.6 41.8 %shard_map.112 = (bf16[1,128,512]{2,1,0:T(8,128)(2,1)S(1)}, f32[32,256]{1,0:T(8,128)S(1)}, f32[32,256]{1,0:T(8,128)S(1)}) custom-call(bf16[1,128,512]{2,1,0:T(8,128)(2,1)} %emb_in.1, s32[1,512]{1,0:T(1,128)} %vis_in.1, s32[1,2048]{1,0:T(1,128)} %win_in.1, bf16[1,128,512]{2,1,0:T(8,128)(2,1)} %og_in.1, f32[1,512]{1,0:T(1,128)} %bitcast.1, ...), custom_call_target="tpu_custom_call" | custom-call | tf_op jit(solution)/shard_map/pallas_call | solution.py:486
  42.4 0.7 %copy.15 = bf16[1,128,512]{2,1,0:T(8,128)(2,1)} copy(bf16[1,128,512]{2,1,0:T(8,128)(2,1)S(1)} %get-tuple-element.6) | data formatting | bytes 262144
  43.1 0.6 %copy.16 = f32[32,256]{1,0:T(8,128)} copy(f32[32,256]{1,0:T(8,128)S(1)} %get-tuple-element.7) | data formatting | bytes 65536
  43.7 0.6 %copy.17 = f32[32,256]{1,0:T(8,128)} copy(f32[32,256]{1,0:T(8,128)S(1)} %get-tuple-element.8) | data formatting | bytes 65536

commit v8 on v7

--- a/solution.py
+++ b/solution.py
@@ -435,12 +435,12 @@
 
     dec_ctx = window_context((parts_mid[2], parts_a[2], parts_b[2]))
     near_columns(dec_ctx, dec_a_send, mm_tn)
-    near_start(1, dec_a_send, dec_a, False)
     grad_enc = from_slots(by_token, all_to_all_wait(2))
     grad_enc_b = grad_enc.astype(BF)
     for j in range(slides):
         enc_b_send[j] = grad_enc_b[:, j * cw : (j + 1) * cw]
     near_start(3, enc_b_send, enc_b, True)
+    near_start(1, dec_a_send, dec_a, False)
     dox = spread(mm_nt(grad_enc_b, enc_out[...]).astype(BF))
     dp = mm_nt(v, dox)
     dsb = (enc_p * (dp - jnp.sum(enc_p * dp, axis=0, keepdims=True)) * scale).astype(BF)

time: 44.5 us -> 47.1 us (1.058)
  Pallas kernels: 41.8 us -> 44.4 us
    pallas_call x1, Pallas kernels: 41.8 us -> 44.4 us  [shards(): pl.pallas_call(functools.partial(kernel, groups, slides, near), out_shape...]
where the time goes in v8:
time: 47.1 us; the launch traced here: 46.9 us
  Pallas kernels  44.4 us (94%)
  local copies, waits for them, and re-layouts  1.89 us (4%)
  between operations  0.64 us (1%)
    pallas_call x1, Pallas kernels, shards(): pl.pallas_call(functools.partial(kernel, groups, slides, near), out_shape...  44.4 us
    unnamed x3, local copies, waits for them, and re-layouts  1.89 us

profile of v8, /device:TPU:0, one launch (start us, length us, event | category | flops | bytes accessed | tf_op | source)
XLA Modules:
  0.0 46.9 jit_solution(440614167717903174)
XLA Ops:
  0.6 44.4 %shard_map.112 = (bf16[1,128,512]{2,1,0:T(8,128)(2,1)S(1)}, f32[32,256]{1,0:T(8,128)S(1)}, f32[32,256]{1,0:T(8,128)S(1)}) custom-call(bf16[1,128,512]{2,1,0:T(8,128)(2,1)} %emb_in.1, s32[1,512]{1,0:T(1,128)} %vis_in.1, s32[1,2048]{1,0:T(1,128)} %win_in.1, bf16[1,128,512]{2,1,0:T(8,128)(2,1)} %og_in.1, f32[1,512]{1,0:T(1,128)} %bitcast.1, ...), custom_call_target="tpu_custom_call" | custom-call | tf_op jit(solution)/shard_map/pallas_call | solution.py:486
  45.0 0.7 %copy.15 = bf16[1,128,512]{2,1,0:T(8,128)(2,1)} copy(bf16[1,128,512]{2,1,0:T(8,128)(2,1)S(1)} %get-tuple-element.6) | data formatting | bytes 262144
  45.7 0.6 %copy.16 = f32[32,256]{1,0:T(8,128)} copy(f32[32,256]{1,0:T(8,128)S(1)} %get-tuple-element.7) | data formatting | bytes 65536
  46.3 0.6 %copy.17 = f32[32,256]{1,0:T(8,128)} copy(f32[32,256]{1,0:T(8,128)S(1)} %get-tuple-element.8) | data formatting | bytes 65536
